TPU v7x, 512 devices: a whole 4x8x8 slice. The times are simulated.
512 devices in a mesh: seq: 128 (over z, y, x_hi), tp: 4 (over x_lo, core).
Axes of the slice: x: 4 (x_hi: 2, x_lo: 2; x = x_hi * 2 + x_lo), y: 8, z: 8, core: 2. Of those that a mesh axis runs over, the one named last changes fastest.
Arguments:
- queries: bfloat16 [32768, 1024], P('seq', 'tp'), may hold values from -6 to 6
- keys: bfloat16 [32768, 1024], P('seq', 'tp'), may hold values from -6 to 6
- values: bfloat16 [32768, 1024], P('seq', 'tp'), may hold values from -6 to 6
- out_weight: bfloat16 [1024, 1024], P('tp'), may hold values from -0.1875 to 0.1875
- out_grad: bfloat16 [32768, 1024], P('seq', 'tp'), may hold values from -6 to 6
- near_offsets: int32 [512, 3], P('seq'), may hold values from -2 to 2, as said below
- coupling: int32 [512, 16], P('seq'), may hold values from 0 to 127
Outputs:
- mixed: bfloat16 [32768, 1024], P('seq', 'tp')
- grad_queries: bfloat16 [32768, 1024], P('seq', 'tp')
- grad_keys: bfloat16 [32768, 1024], P('seq', 'tp')
- grad_values: bfloat16 [32768, 1024], P('seq', 'tp')
- grad_weight: float32 [1024, 1024], P('tp')
Inputs may be any that keep to these rules, and one draw needn't show every extreme that they name: `near_offsets`: each block's row holds 0 and two different nonzero offsets.
All inputs are finite; a program needn't handle non-finite values.
Results may differ from a plain program's by a relative error of at most 0.017.
Values may be sent and summed in bfloat16 or wider, within the bound.
A program may use at most 64 MiB of HBM per device.

v0:
```python
import math

import jax
import jax.numpy as jnp
from jax import lax
from jax.sharding import PartitionSpec as P

HD = 64
NB = 64
GROUP = 4


def with_halo(block, sides, width):
    for axis, dim in sides:
        count = lax.axis_size(axis)
        forward = [(i, i + 1) for i in range(count - 1)]
        backward = [(target, source) for source, target in forward]
        low = lax.ppermute(
            lax.slice_in_dim(block, block.shape[dim] - width, None, axis=dim), axis, forward
        )
        high = lax.ppermute(lax.slice_in_dim(block, 0, width, axis=dim), axis, backward)
        block = jnp.concatenate([low, block, high], axis=dim)
    return block


def from_behind(shard, axis, by):
    peers = lax.axis_size(axis)
    pairs = [(i, i + by) for i in range(peers) if 0 <= i + by < peers]
    return lax.ppermute(shard, axis, pairs)


def group_sum(fine_rows):
    col_count = fine_rows.shape[1]
    summed = jnp.sum(fine_rows.astype(jnp.float32).reshape(-1, GROUP, col_count), 1)
    return (summed / math.sqrt(GROUP)).astype(jnp.bfloat16)


def shards(queries, keys, values, out_weight, out_grad, near_offsets, coupling):
    tok_count, feat_cols = keys.shape
    head_count = feat_cols // HD
    block_count = tok_count // NB
    seq_index = lax.axis_index("seq")
    total_blocks = lax.axis_size("seq") * block_count
    root_dim = math.sqrt(HD)
    key_vals = jnp.concatenate([keys, values], 1)
    padded = with_halo(key_vals, (("seq", 0),), 2 * NB)
    padded = padded.reshape(block_count + 4, NB, 2 * feat_cols)
    fine_own = (
        jnp.sum(key_vals.astype(jnp.float32).reshape(block_count, NB, 2 * feat_cols), 1)
        / math.sqrt(NB)
    ).astype(jnp.bfloat16)
    fine_all = lax.all_gather(fine_own, "seq", axis=0, tiled=True)
    top_rows = lax.all_gather(group_sum(fine_own), "seq", axis=0, tiled=True)
    tile_rows = fine_all.reshape(-1, GROUP, 2 * feat_cols)
    block_ids = jnp.arange(block_count, dtype=jnp.int32)[:, None]
    near_rows = padded[block_ids + near_offsets + 2].reshape(block_count, 3 * NB, 2 * feat_cols)
    far_rows = tile_rows[coupling].reshape(block_count, -1, 2 * feat_cols)
    local_rows = jnp.concatenate([near_rows, far_rows], 1)
    local_count = local_rows.shape[1]
    target = seq_index * block_count + block_ids + near_offsets
    inside = (target >= 0) & (target < total_blocks)
    usable = jnp.concatenate(
        [jnp.repeat(inside, NB, axis=1), jnp.ones((block_count, local_count - 3 * NB), bool)], 1
    )
    query_blks = queries.reshape(block_count, NB, head_count, HD)
    local_keys = local_rows[:, :, :feat_cols].reshape(block_count, local_count, head_count, HD)
    local_vals = local_rows[:, :, feat_cols:].reshape(block_count, local_count, head_count, HD)
    top_keys = top_rows[:, :feat_cols].reshape(-1, head_count, HD)
    top_vals = top_rows[:, feat_cols:].reshape(-1, head_count, HD)
    near_scores = (
        jnp.einsum("bqhd,bkhd->bhqk", query_blks, local_keys, preferred_element_type=jnp.float32)
        / root_dim
    )
    near_scores = jnp.where(usable[:, None, None, :], near_scores, -jnp.inf)
    top_scores = (
        jnp.einsum("bqhd,khd->bhqk", query_blks, top_keys, preferred_element_type=jnp.float32)
        / root_dim
    )
    scores = jnp.concatenate([near_scores, top_scores], 3)
    row_peak = jnp.max(scores, 3, keepdims=True)
    exp_scores = jnp.exp(scores - row_peak)
    attn_prob = exp_scores / jnp.sum(exp_scores, 3, keepdims=True)
    prob_half = attn_prob.astype(jnp.bfloat16)
    attended = jnp.einsum(
        "bhqk,bkhd->bqhd",
        prob_half[..., :local_count],
        local_vals,
        preferred_element_type=jnp.float32,
    ) + jnp.einsum(
        "bhqk,khd->bqhd", prob_half[..., local_count:], top_vals, preferred_element_type=jnp.float32
    )
    attended = attended.reshape(tok_count, feat_cols).astype(jnp.bfloat16)
    partial_out = jnp.dot(attended, out_weight, preferred_element_type=jnp.float32)
    mixed = lax.psum_scatter(partial_out, "tp", scatter_dimension=1, tiled=True).astype(
        jnp.bfloat16
    )
    shard_cols = lax.all_gather(out_grad, "tp", axis=1, tiled=True)
    grad_attn = jnp.einsum("tn,wn->tw", shard_cols, out_weight, preferred_element_type=jnp.float32)
    update = jnp.einsum("tw,tn->wn", attended, shard_cols, preferred_element_type=jnp.float32)
    grad_attn, grad_part = (grad_attn, update)
    grad_weight = lax.psum(grad_part, "seq")
    grad_out = grad_attn.astype(jnp.bfloat16).reshape(block_count, NB, head_count, HD)
    dprob = jnp.concatenate(
        [
            jnp.einsum("bqhd,bkhd->bhqk", grad_out, local_vals, preferred_element_type=jnp.float32),
            jnp.einsum("bqhd,khd->bhqk", grad_out, top_vals, preferred_element_type=jnp.float32),
        ],
        3,
    )
    inner = jnp.sum(attn_prob * dprob, 3, keepdims=True)
    dscore = (attn_prob * (dprob - inner) / root_dim).astype(jnp.bfloat16)
    grad_queries = jnp.einsum(
        "bhqk,bkhd->bqhd", dscore[..., :local_count], local_keys, preferred_element_type=jnp.float32
    ) + jnp.einsum(
        "bhqk,khd->bqhd", dscore[..., local_count:], top_keys, preferred_element_type=jnp.float32
    )
    grad_queries = grad_queries.reshape(tok_count, feat_cols).astype(jnp.bfloat16)
    local_kgrad = jnp.einsum(
        "bhqk,bqhd->bkhd", dscore[..., :local_count], query_blks, preferred_element_type=jnp.float32
    )
    local_vgrad = jnp.einsum(
        "bhqk,bqhd->bkhd",
        prob_half[..., :local_count],
        grad_out,
        preferred_element_type=jnp.float32,
    )
    top_kgrad = jnp.einsum(
        "bhqk,bqhd->khd", dscore[..., local_count:], query_blks, preferred_element_type=jnp.float32
    )
    top_vgrad = jnp.einsum(
        "bhqk,bqhd->khd", prob_half[..., local_count:], grad_out, preferred_element_type=jnp.float32
    )
    local_grads = jnp.concatenate(
        [
            local_kgrad.reshape(block_count, local_count, feat_cols),
            local_vgrad.reshape(block_count, local_count, feat_cols),
        ],
        2,
    )
    top_grads = jnp.concatenate(
        [top_kgrad.reshape(-1, feat_cols), top_vgrad.reshape(-1, feat_cols)], 1
    )
    near_grads = local_grads[:, : 3 * NB].reshape(block_count, 3, NB, 2 * feat_cols)
    grad_pad = (
        jnp.zeros((block_count + 4, NB, 2 * feat_cols), jnp.float32)
        .at[block_ids + near_offsets + 2]
        .add(near_grads)
    )
    lower_part = grad_pad[:2].reshape(2 * NB, 2 * feat_cols)
    upper_part = grad_pad[-2:].reshape(2 * NB, 2 * feat_cols)
    from_above = from_behind(lower_part.astype(jnp.bfloat16), "seq", -1).astype(lower_part.dtype)
    from_below = from_behind(upper_part.astype(jnp.bfloat16), "seq", 1).astype(upper_part.dtype)
    grad_tokens = grad_pad[2:-2].reshape(tok_count, 2 * feat_cols)
    grad_tokens = grad_tokens.at[: 2 * NB].add(from_below).at[tok_count - 2 * NB :].add(from_above)
    far_grads = local_grads[:, 3 * NB :].reshape(block_count, -1, GROUP, 2 * feat_cols)
    fine_terms = (
        jnp.zeros((total_blocks // GROUP, GROUP, 2 * feat_cols), jnp.float32)
        .at[coupling]
        .add(far_grads)
    )
    fine_terms = fine_terms.reshape(total_blocks, 2 * feat_cols)
    grad_fine = lax.psum_scatter(fine_terms, "seq", scatter_dimension=0, tiled=True)
    grad_top = lax.psum_scatter(top_grads, "seq", scatter_dimension=0, tiled=True)
    grad_fine = grad_fine + jnp.repeat(grad_top / math.sqrt(GROUP), GROUP, axis=0)
    grad_tokens = grad_tokens + jnp.repeat(grad_fine / math.sqrt(NB), NB, axis=0)
    return (
        mixed,
        grad_queries,
        grad_tokens[:, :feat_cols].astype(jnp.bfloat16),
        grad_tokens[:, feat_cols:].astype(jnp.bfloat16),
        grad_weight,
    )


def solution(mesh):
    in_specs = (
        P("seq", "tp"),
        P("seq", "tp"),
        P("seq", "tp"),
        P("tp", None),
        P("seq", "tp"),
        P("seq", None),
        P("seq", None),
    )
    out_specs = (P("seq", "tp"), P("seq", "tp"), P("seq", "tp"), P("seq", "tp"), P("tp", None))
    return jax.shard_map(shards, mesh=mesh, in_specs=in_specs, out_specs=out_specs, check_vma=False)
```

profile of v0, /device:TPU:6, one launch (start us, length us, event | category | flops | bytes accessed | tf_op | source)
XLA Modules:
  0.0 2134.7 jit_solution(13851578553587800458)
XLA Ops:
  8.1 1.0 constant_dynamic-update-slice_fusion.1
  9.1 0.9 constant_dynamic-update-slice_fusion
  10.0 0.7 fusion.39
  10.7 4.3 collective-permute-start
  15.0 3.7 collective-permute-start.1
  18.7 1.1 reshape.175
  19.8 0.2 copy.85
  20.3 0.4 copy-done.19
  20.7 358.7 %all-gather.1 = bf16[128,4,512]{2,1,0:T(4,128)(2,1)S(1)} all-gather(bf16[1,4,512]{2,1,0:T(4,128)(2,1)S(1)} %get-tuple-element.43), channel_id=1, replica_groups=mesh['seq'=128,'tp'=4] {'seq'}, dimensions={0}, use_global_device_ids=true | all-gather | bytes 528384 | tf_op jit(solution)/shard_map/all_gather | solution.py:52
  379.5 0.8 gather_fusion.1
  380.6 354.5 %all-gather.2 = bf16[128,1,512]{2,1,0:T(2,128)(2,1)S(1)} all-gather(bf16[1,1,512]{2,1,0:T(2,128)(2,1)S(1)} %reshape.237), channel_id=2, replica_groups=mesh['seq'=128,'tp'=4] {'seq'}, dimensions={0}, use_global_device_ids=true | all-gather | bytes 132096 | tf_op jit(solution)/shard_map/all_gather | solution.py:53
  735.3 0.2 fusion.45
  735.6 6.6 all_gather.11
  742.2 0.8 copy-done.3
  743.0 0.3 convolution_convert_fusion
  743.9 1.1 convolution_bitcast_fusion.1
  744.9 0.2 fusion.34
  745.2 1.0 pad_maximum_fusion.4
  746.2 0.6 gather_fusion
  746.8 0.9 pad_maximum_fusion.3
  747.7 1.2 copy.75
  748.9 0.2 copy.74
  749.1 1.3 fusion.43
  750.5 0.4 fusion.41
  751.0 0.5 fusion.13
  751.5 1.4 fusion.36
  752.9 0.3 convolution_bitcast_fusion.4
  753.2 0.4 fusion.11
  753.6 0.2 copy.81
  753.8 0.2 convert_element_type.75
  754.0 1.3 fusion.42
  755.3 0.2 all-reduce.6.cloned.1.call-start
  755.6 7.9 multiply_convert_fusion
  763.5 1.3 fusion.17
  764.8 1.6 copy.87
  766.4 1.3 fusion.20
  767.6 1.6 copy.88
  769.2 0.9 pad_maximum_fusion.2
  770.1 2.0 reshape.218
  772.1 1.1 broadcast_in_dim.45
  773.2 8.8 scatter_fusion.1
  782.0 2.6 reshape.185
  784.5 1.9 fusion.27
  786.4 1.7 copy.92
  788.1 1.8 fusion.24
  789.9 1.0 copy.93
  790.9 1.6 pad_maximum_fusion.5
  792.6 2.3 fusion.44
  794.9 1.3 dynamic-slice.16
  796.9 1.4 fusion.1
  798.4 3.1 scatter_fusion
  801.7 2.1 collective-permute-start.2
  803.8 5.4 collective-permute-start.3
  809.3 0.3 convolution_bitcast_fusion.3
  809.6 0.4 fusion.10
  809.9 0.2 copy.84
  810.1 0.9 convert_element_type.80
  811.0 3.6 collective-permute-done.2
  814.7 1.6 convert_element_type.76
  816.3 1307.0 %all-reduce.6.cloned.1.call-done = (f32[512,512]{1,0:T(8,128)}, f32[128,512]{1,0:T(8,128)}, f32[256,1024]{1,0:T(8,128)}) async-done(((f32[512,512]{1,0:T(8,128)}, f32[128,512]{1,0:T(8,128)}, f32[256,1024]{1,0:T(8,128)}), (f32[512,512]{1,0:T(8,128)}, f32[128,512]{1,0:T(8,128)}, f32[256,1024]{1,0:T(8,128)})) %all-reduce.6.cloned.1.call-update) | async-done | bytes 2359312
  2123.3 1.5 dynamic-slice_multiply_fusion
  2124.8 0.7 fusion.30
  2125.6 0.7 fusion.38
  2126.3 1.0 copy.115
  (88 shorter events, 1.9 us)
Async XLA Ops:
  8.0 735.0 %copy-start = (bf16[256,1024]{1,0:T(8,128)(2,1)S(1)}, bf16[256,1024]{1,0:T(8,128)(2,1)}, u32[]{:S(2)}) copy-start(bf16[256,1024]{1,0:T(8,128)(2,1)} %param.14) | copy-start | bytes 1572868
  8.0 12.2 copy-start.17
  8.0 12.1 copy-start.16
  8.0 12.0 copy-start.23
  8.0 806.7 %reduce-scatter.2.cloned.1.call-start = ((), (), s32[]{:S(2)}) async-start(), calls=%async_computation.1 | async-start | bytes 1310720 | tf_op jit(solution)/shard_map/reduce_scatter | solution.py:94
  9.1 370.3 %copy-start.24 = (s32[4,16]{1,0:T(4,128)S(1)}, s32[4,16]{1,0:T(4,128)}, u32[]{:S(2)}) copy-start(s32[4,16]{1,0:T(4,128)} %param.17) | copy-start | bytes 772
  10.7 734.5 %collective-permute-start = (bf16[128,512]{1,0:T(8,128)(2,1)}, bf16[128,512]{1,0:T(8,128)(2,1)}, u32[]{:S(2)}, u32[]{:S(2)}) collective-permute-start(bf16[128,512]{1,0:T(8,128)(2,1)} %get-tuple-element.38), channel_id=1, source_target_pairs={{0,4},{4,8},{8,12},{12,16},{16,20},{20,24},{24,28},{28,32},{32,36}... | collective-permute-start | bytes 393224 | tf_op jit(solution)/shard_map/ppermute | solution.py:18
  15.0 730.1 %collective-permute-start.1 = (bf16[128,512]{1,0:T(8,128)(2,1)S(1)}, bf16[128,512]{1,0:T(8,128)(2,1)}, u32[]{:S(2)}, u32[]{:S(2)}) collective-permute-start(bf16[128,512]{1,0:T(8,128)(2,1)S(1)} %get-tuple-element.39), channel_id=1, source_target_pairs={{4,0},{8,4},{12,8},{16,12},{20,16},{24,20},{28,24},{32,28},{36,32}... | collective-permute-start | bytes 393224 | tf_op jit(solution)/shard_map/ppermute | solution.py:21
  20.0 730.5 %copy-start.6 = (bf16[4,64,4,64]{1,3,2,0:T(8,128)(2,1)}, bf16[4,64,4,64]{1,3,2,0:T(8,128)(2,1)S(1)}, u32[]{:S(2)}) copy-start(bf16[4,64,4,64]{1,3,2,0:T(8,128)(2,1)S(1)} %copy.85) | copy-start | bytes 393220
  20.2 0.5 copy-start.19
  379.4 355.9 %copy-start.21 = (s32[64]{0:T(128)}, s32[64]{0:T(128)S(1)}, u32[]{:S(2)}) copy-start(s32[64]{0:T(128)S(1)} %reshape.200) | copy-start | bytes 772
  380.3 355.2 %copy-start.18 = (bf16[256,256]{1,0:T(8,128)(2,1)S(1)}, bf16[256,256]{1,0:T(8,128)(2,1)}, u32[]{:S(2)}) copy-start(bf16[256,256]{1,0:T(8,128)(2,1)} %param.15) | copy-start | bytes 393220
  735.3 6.9 copy-start.14
  735.6 15.4 copy-start.4
  742.2 0.8 copy-start.3
  743.5 2.7 copy-start.13
  743.7 5.4 copy-start.8
  748.9 2.0 copy-start.1
  753.8 1.8 copy-start.5
  755.3 8.2 copy-start.7
  755.3 1368.0 %all-reduce.6.cloned.1.call-start = ((), (), s32[]{:S(2)}) async-start(), calls=%async_computation.2 | async-start | bytes 4718592
  763.5 1.3 copy-start.10
  763.5 2.9 copy-start.9
  770.1 3.1 copy-start.22
  796.9 1.5 copy-start.20
  801.5 7.7 copy-start.2
  801.5 7.7 copy-start.11
  801.7 7.9 copy-start.15
  801.7 12.8 collective-permute-start.2
  803.8 10.8 collective-permute-start.3
  2123.3 3.0 copy-start.12
Sparse Core Ops, SparseCore 0:
  755.4 16.0 reduce-scatter.1
Sparse Core Ops, SparseCore 1:
  795.0 1328.3 all-reduce.5
where the time goes:
time: 2140 us; the launch traced here: 2130 us
  waiting for transfers between devices  1310 us (61%)
  blocking collectives  720 us (34%)
  other arithmetic  32 us (1%)
  local copies, waits for them, and re-layouts  25.2 us (1%)
    unnamed x3, waiting for transfers between devices  1310 us
    all_gather x1, blocking collectives, shards(): fine_all = lax.all_gather(fine_own, 'seq', axis=0, tiled=True)  359 us
    all_gather x1, blocking collectives, shards(): top_rows = lax.all_gather(group_sum(fine_own), 'seq', axis=0, tiled=True)  355 us
  transfers between devices with their start and end apart: 6, of which 2 were waited for; matrix products, arithmetic and copies ran while one was open for 3% of the time, Pallas kernels for 0%

commit v1 on v0

v1 whole, which is shorter than its diff:
```python
import functools

import jax
import jax.numpy as jnp
from jax import lax
from jax.experimental import pallas as pl
from jax.experimental.pallas import tpu as pltpu
from jax.sharding import PartitionSpec as P

MESH = pl.DeviceIdType.MESH
F32 = jnp.float32
BF16 = jnp.bfloat16
HD = 64
NB = 64
BLK = 4
HEADS = 4
COLS = HEADS * HD
TOK = BLK * NB
C1 = 16
LANE = 128
SUB = 16
NEAR = 5 * NB
FAR = C1 * BLK


def each(low, high, body):
    lax.fori_loop(low, high, lambda k, c: (body(k), c)[1], 0)


def dot_nn(a, b):
    return lax.dot_general(a, b, (((1,), (0,)), ((), ())), preferred_element_type=F32)


def dot_nt(a, b):
    return lax.dot_general(a, b, (((1,), (1,)), ((), ())), preferred_element_type=F32)


def dot_tn(a, b):
    return lax.dot_general(a, b, (((0,), (0,)), ((), ())), preferred_element_type=F32)


def iota(shape, dim):
    return lax.broadcasted_iota(jnp.int32, shape, dim)


class Place:
    def __init__(self, n, tps):
        self.n, self.tps = n, tps
        self.seqs = 2 * n * n
        self.seq = lax.axis_index("seq")
        self.tp = lax.axis_index("tp")
        self.z = lax.div(self.seq, 2 * n)
        self.y = lax.rem(lax.div(self.seq, 2), n)
        self.xh = lax.rem(self.seq, 2)
        self.mine = self.z * (1 - self.xh) + self.y * self.xh
        self.cross = self.y * (1 - self.xh) + self.z * self.xh
        self.spot = self.xh * n * n + self.cross * n + self.mine

    def at(self, z, y, xh):
        return (z * (2 * self.n) + y * 2 + xh, self.tp)

    def along_mine(self, k, xh):
        c = lax.rem(self.mine + k, self.n)
        return self.at(
            c * (1 - self.xh) + self.z * self.xh, self.y * (1 - self.xh) + c * self.xh, xh
        )

    def along_cross(self, k, xh):
        c = lax.rem(self.cross + k, self.n)
        return c, self.at(
            self.z * (1 - self.xh) + c * self.xh, c * (1 - self.xh) + self.y * self.xh, xh
        )

    def along_y(self, k):
        c = lax.rem(self.y + k, self.n)
        return c, self.at(self.z, c, self.xh)

    def along_z(self, k):
        c = lax.rem(self.z + k, self.n)
        return c, self.at(c, self.y, self.xh)

    def step(self, by):
        return (lax.rem(self.seq + self.seqs + by, self.seqs), self.tp)

    def tp_at(self, k):
        c = lax.rem(self.tp + k, self.tps)
        return c, (self.seq, c)


def remote(src, dst, send, recv, device):
    return pltpu.make_async_remote_copy(
        src_ref=src, dst_ref=dst, send_sem=send, recv_sem=recv, device_id=device, device_id_type=MESH
    )


def gather_1(w, buf, send, recv, act):
    def same(k):
        act(remote(buf.at[w.spot], buf.at[w.spot], send.at[0, k], recv.at[0, k], w.along_mine(k, w.xh)))

    def other(k):
        act(remote(buf.at[w.spot], buf.at[w.spot], send.at[1, k], recv.at[1, k], w.along_mine(k, 1 - w.xh)))

    each(1, w.n, same)
    each(0, w.n, other)


def gather_2(w, buf, send, recv, act):
    n = w.n

    def one(k):
        rows = buf.at[pl.ds(w.y * n, n)]
        act(remote(rows, rows, send.at[0, k], recv.at[0, k], w.along_y(k)[1]))
        rows = buf.at[pl.ds(n * n + w.z * n, n)]
        act(remote(rows, rows, send.at[1, k], recv.at[1, k], w.along_z(k)[1]))

    each(1, n, one)


def scatter_1(w, part, got, send, recv, act):
    n = w.n

    def one(k):
        c, device = w.along_y(k)
        act(remote(part.at[pl.ds(c * n, n)], got.at[0, k], send.at[0, k], recv.at[0, k], device))
        c, device = w.along_z(k)
        act(remote(part.at[pl.ds(n * n + c * n, n)], got.at[1, k], send.at[1, k], recv.at[1, k], device))

    each(1, n, one)


def reduce_1(w, part, got, rows):
    n = w.n
    for half, row in ((0, w.y), (1, w.z)):
        total = part[pl.ds(half * n * n + row * n, n)].astype(F32)
        for k in range(1, n):
            total += got[half, k].astype(F32)
        rows[half] = total.astype(BF16)


def scatter_2(w, rows, got, send, recv, act):
    def same(k):
        c = lax.rem(w.mine + k, w.n)
        act(remote(rows.at[w.xh, c], got.at[0, k], send.at[0, k], recv.at[0, k], w.along_mine(k, w.xh)))

    def other(k):
        c, device = w.along_cross(k, 1 - w.xh)
        act(remote(rows.at[1 - w.xh, c], got.at[1, k], send.at[1, k], recv.at[1, k], device))

    each(1, w.n, same)
    each(0, w.n, other)


def reduce_2(w, rows, got):
    total = rows[w.xh, w.mine].astype(F32)
    for k in range(1, w.n):
        total += got[0, k].astype(F32)
    for k in range(w.n):
        total += got[1, k].astype(F32)
    return total


def start(copy):
    copy.start()


def landed(copy):
    copy.wait_recv()


def sent(copy):
    copy.wait_send()


def kernel(
    n, tps, group,
    off_ref, cpl_ref, q_ref, k_ref, v_ref, w_ref, og_ref,
    mixed_ref, gq_ref, gk_ref, gv_ref, gw_ref,
    kpad, vpad, fine, ogs, kft, vft, hot, probs, halves, att, gatt, mine_out,
    msend, mgot, gkpad, gvpad, hsend, hgot, dlist, dtop,
    wpart, wgot1, wrows, wgot2, wfull, fpart, fgot1, frows, fgot2,
    s_g1, r_g1, s_g2, r_g2, s_h, r_h, s_o, r_o, s_m, r_m, s_b, r_b,
    s_w1, r_w1, s_w2, r_w2, s_w3, r_w3, s_w4, r_w4, s_f1, r_f1, s_f2, r_f2,
):
    w = Place(n, tps)
    tiles = w.seqs
    groups = tiles // group
    nblk = tiles * BLK

    barrier = pltpu.get_barrier_semaphore()

    def greet(device):
        pl.semaphore_signal(barrier, inc=1, device_id=device, device_id_type=MESH)

    def greet_square(k):
        greet(w.along_y(k)[1])
        greet(w.along_z(k)[1])
        greet(w.along_mine(k, 1 - w.xh))
        greet(w.along_cross(k, 1 - w.xh)[1])

    each(1, n, greet_square)
    greet(w.at(w.z, w.y, 1 - w.xh))
    greet(w.step(1))
    greet(w.step(-1))
    each(1, tps, lambda k: greet(w.tp_at(k)[1]))

    piece = jnp.zeros((SUB, LANE), F32)
    for c in range(4):
        row, tok = iota((SUB, TOK), 0), iota((SUB, TOK), 1)
        pick = jnp.where((row - c * BLK) == (tok >> 6), 1.0, 0.0).astype(BF16)
        src = k_ref if c < 2 else v_ref
        piece += dot_nn(pick, src[:, (c % 2) * LANE : (c % 2 + 1) * LANE])
    fine[w.spot] = (piece * 0.125).astype(BF16)
    ogs[w.tp] = og_ref[...]
    pl.semaphore_wait(barrier, 4 * (n - 1) + 3 + tps - 1)

    half = TOK // 2

    def halo(act):
        for i, (src, pad) in enumerate(((k_ref, kpad), (v_ref, vpad))):
            act(remote(src.at[pl.ds(half, half)], pad.at[pl.ds(0, half)], s_h.at[i], r_h.at[i], w.step(1)))
            act(remote(src.at[pl.ds(0, half)], pad.at[pl.ds(half + TOK, half)], s_h.at[2 + i], r_h.at[2 + i], w.step(-1)))

    def columns(act):
        def one(k):
            act(remote(og_ref, ogs.at[w.tp], s_o.at[k], r_o.at[k], w.tp_at(k)[1]))

        each(1, tps, one)

    gather_1(w, fine, s_g1, r_g1, start)
    halo(start)
    columns(start)

    kpad[half : half + TOK] = k_ref[...]
    vpad[half : half + TOK] = v_ref[...]
    gkpad[...] = jnp.zeros_like(gkpad)
    gvpad[...] = jnp.zeros_like(gvpad)
    dtop[...] = jnp.zeros_like(dtop)

    spot = iota((1, tiles), 1)
    in_square, bits = spot & (n * n - 1), n.bit_length() - 1
    a, c = in_square >> bits, in_square & (n - 1)
    tile_of = jnp.where(spot < n * n, c * (2 * n) + a * 2, a * (2 * n) + c * 2 + 1)
    rows8 = iota((8, tiles), 0)
    listed = []
    for g in range(BLK * C1 // 8):
        wanted = jnp.zeros((8, tiles), jnp.int32)
        for i in range(8):
            at = g * 8 + i
            wanted = jnp.where(rows8 == i, cpl_ref[at // C1, at % C1], wanted)
        listed.append(wanted)
    wanted = jnp.concatenate(listed, 0)
    hot[...] = jnp.where(wanted == tile_of, 1.0, 0.0).astype(BF16)

    size = group * SUB
    to, fro = iota((size, size), 0), iota((size, size), 1)
    gbits = group.bit_length() - 1
    swapped = (fro & (SUB - 1)) * group + (fro >> 4)
    swap = jnp.where(to == swapped, 1.0, 0.0).astype(BF16)
    swapped = (fro & (group - 1)) * SUB + (fro >> gbits)
    swap_back = jnp.where(to == swapped, 1.0, 0.0).astype(BF16)

    head_of = iota((1, COLS), 1) >> 6
    masks = [jnp.where(head_of == h, 1.0, 0.0) for h in range(HEADS)]
    masks_b = [m.astype(BF16) for m in masks]

    def diagonal(rows):
        return jnp.concatenate([rows * m for m in masks_b], 0)

    def collect(full):
        out = full[0:NB] * masks[0]
        for h in range(1, HEADS):
            out += full[h * NB : (h + 1) * NB] * masks[h]
        return out

    gather_1(w, fine, s_g1, r_g1, landed)
    gather_2(w, fine, s_g2, r_g2, start)
    halo(landed)
    gather_2(w, fine, s_g2, r_g2, landed)

    packed = jnp.concatenate([fine[g * group : (g + 1) * group].reshape(size, LANE) for g in range(groups)], 1)
    by_row = dot_nn(swap, packed)
    flat = jnp.concatenate(
        [
            jnp.concatenate([by_row[s * group : (s + 1) * group, g * LANE : (g + 1) * LANE] for s in range(SUB)], 1)
            for g in range(groups)
        ],
        0,
    )
    tops = []
    for c in range(4):
        total = flat[:, c * BLK * LANE : (c * BLK + 1) * LANE]
        for r in range(1, BLK):
            total += flat[:, (c * BLK + r) * LANE : (c * BLK + r + 1) * LANE]
        tops.append((total * 0.5).astype(BF16))
    far = dot_nn(hot[...], flat.astype(BF16)).astype(BF16)
    for b in range(BLK):
        for r in range(BLK):
            for c in range(4):
                s = c * BLK + r
                into = kft if c < 2 else vft
                into[b, r * C1 : (r + 1) * C1, (c % 2) * LANE : (c % 2 + 1) * LANE] = far[
                    b * C1 : (b + 1) * C1, s * LANE : (s + 1) * LANE
                ]
        kft[b, FAR:, :LANE], kft[b, FAR:, LANE:] = tops[0], tops[1]
        vft[b, FAR:, :LANE], vft[b, FAR:, LANE:] = tops[2], tops[3]

    def listed_rows(pad, rest, b):
        return jnp.concatenate([pad[b * NB : b * NB + NEAR], rest[b]], 0)

    for b in range(BLK):
        keys = listed_rows(kpad, kft, b)
        vals = listed_rows(vpad, vft, b)
        scores = dot_nt(keys, diagonal(q_ref[b * NB : (b + 1) * NB])) * 0.125
        parts = []
        for d in range(5):
            target = w.seq * BLK + b + d - 2
            chosen = (off_ref[b, 0] == d - 2) | (off_ref[b, 1] == d - 2) | (off_ref[b, 2] == d - 2)
            usable = chosen & (target >= 0) & (target < nblk)
            parts.append(scores[d * NB : (d + 1) * NB] + jnp.where(usable, 0.0, -1e30))
        scores = jnp.concatenate(parts + [scores[NEAR:]], 0)
        peak = jnp.max(scores, 0, keepdims=True)
        exps = jnp.exp(scores - peak)
        prob = exps * (1.0 / jnp.sum(exps, 0, keepdims=True))
        prob_b = prob.astype(BF16)
        probs[b] = prob
        halves[b] = prob_b
        att[b * NB : (b + 1) * NB] = collect(dot_tn(prob_b, vals)).astype(BF16)

    columns(landed)
    for t in range(tps):
        part = dot_tn(att[...], ogs[t]).astype(BF16)
        for j in range(COLS // LANE):
            wpart[(t * 2 + j) * 16 : (t * 2 + j + 1) * 16] = part[:, j * LANE : (j + 1) * LANE].reshape(16, SUB, LANE)
    scatter_1(w, wpart, wgot1, s_w1, r_w1, start)

    for t in range(tps):
        msend[t] = dot_nn(att[...], w_ref[:, t * COLS : (t + 1) * COLS]).astype(BF16)

    def mix(act):
        def one(k):
            c, device = w.tp_at(k)
            act(remote(msend.at[c], mgot.at[k], s_m.at[k], r_m.at[k], device))

        each(1, tps, one)

    mix(start)
    mine_out[...] = dot_nn(att[...], w_ref[:, pl.ds(pl.multiple_of(w.tp * COLS, COLS), COLS)])

    grad = dot_nt(ogs[0], w_ref[:, 0:COLS])
    for t in range(1, tps):
        grad += dot_nt(ogs[t], w_ref[:, t * COLS : (t + 1) * COLS])
    gatt[...] = grad.astype(BF16)

    for b in range(BLK):
        keys = listed_rows(kpad, kft, b)
        vals = listed_rows(vpad, vft, b)
        q_diag = diagonal(q_ref[b * NB : (b + 1) * NB])
        g_diag = diagonal(gatt[b * NB : (b + 1) * NB])
        prob = probs[b]
        dprob = dot_nt(vals, g_diag)
        inner = jnp.sum(prob * dprob, 0, keepdims=True)
        dscore = (prob * (dprob - inner) * 0.125).astype(BF16)
        gq_ref[b * NB : (b + 1) * NB] = collect(dot_tn(dscore, keys)).astype(BF16)
        dkey = dot_nn(dscore, q_diag)
        dval = dot_nn(halves[b], g_diag)
        gkpad[b * NB : b * NB + NEAR] += dkey[:NEAR]
        gvpad[b * NB : b * NB + NEAR] += dval[:NEAR]
        for r in range(BLK):
            for c in range(4):
                s = c * BLK + r
                src = dkey if c < 2 else dval
                dlist[b * C1 : (b + 1) * C1, s * LANE : (s + 1) * LANE] = src[
                    NEAR + r * C1 : NEAR + (r + 1) * C1, (c % 2) * LANE : (c % 2 + 1) * LANE
                ].astype(BF16)
        dtop[:, :COLS] += dkey[NEAR + FAR :]
        dtop[:, COLS:] += dval[NEAR + FAR :]

    for i, pad in enumerate((gkpad, gvpad)):
        hsend[i] = pad[half + TOK :].astype(BF16)
        hsend[2 + i] = pad[:half].astype(BF16)

    def halo_back(act):
        for i in range(2):
            act(remote(hsend.at[i], hgot.at[i], s_b.at[i], r_b.at[i], w.step(1)))
            act(remote(hsend.at[2 + i], hgot.at[2 + i], s_b.at[2 + i], r_b.at[2 + i], w.step(-1)))

    tile_grad = dot_tn(hot[...], dlist[...])
    cols = []
    for c in range(4):
        for r in range(BLK):
            s = c * BLK + r
            cols.append(tile_grad[:, s * LANE : (s + 1) * LANE] + dtop[:, c * LANE : (c + 1) * LANE] * 0.5)
    by_row = jnp.concatenate(
        [
            jnp.concatenate([cols[s][g * group : (g + 1) * group] for s in range(SUB)], 0)
            for g in range(groups)
        ],
        1,
    ).astype(BF16)
    packed = dot_nn(swap_back, by_row).astype(BF16)
    for g in range(groups):
        fpart[g * group : (g + 1) * group] = packed[:, g * LANE : (g + 1) * LANE].reshape(group, SUB, LANE)
    scatter_1(w, fpart, fgot1, s_f1, r_f1, start)
    halo_back(start)

    scatter_1(w, wpart, wgot1, s_w1, r_w1, landed)
    reduce_1(w, wpart, wgot1, wrows)
    scatter_2(w, wrows, wgot2, s_w2, r_w2, start)

    scatter_1(w, fpart, fgot1, s_f1, r_f1, landed)
    reduce_1(w, fpart, fgot1, frows)
    scatter_2(w, frows, fgot2, s_f2, r_f2, start)

    scatter_2(w, wrows, wgot2, s_w2, r_w2, landed)
    wfull[w.spot] = reduce_2(w, wrows, wgot2).astype(BF16)
    gather_1(w, wfull, s_w3, r_w3, start)

    mix(landed)
    total = mine_out[...]
    for k in range(1, tps):
        total += mgot[k].astype(F32)
    mixed_ref[...] = total.astype(BF16)
    halo_back(landed)

    gather_1(w, wfull, s_w3, r_w3, landed)
    gather_2(w, wfull, s_w4, r_w4, start)

    scatter_2(w, frows, fgot2, s_f2, r_f2, landed)
    fine_grad = reduce_2(w, frows, fgot2) * 0.125
    for i, (pad, out) in enumerate(((gkpad, gk_ref), (gvpad, gv_ref))):
        for r in range(BLK):
            rows = pad[half + r * NB : half + (r + 1) * NB]
            if r < BLK // 2:
                rows += hgot[i, r * NB : (r + 1) * NB].astype(F32)
            else:
                rows += hgot[2 + i, r * NB - half : (r + 1) * NB - half].astype(F32)
            for c in range(2):
                s = (2 * i + c) * BLK + r
                out[r * NB : (r + 1) * NB, c * LANE : (c + 1) * LANE] = (
                    rows[:, c * LANE : (c + 1) * LANE] + fine_grad[s : s + 1]
                ).astype(BF16)

    gather_2(w, wfull, s_w4, r_w4, landed)
    for j in range(tps * COLS // LANE):
        gw_ref[:, j * LANE : (j + 1) * LANE] = wfull[j * 16 : (j + 1) * 16].reshape(COLS, LANE).astype(F32)

    gather_1(w, fine, s_g1, r_g1, sent)
    gather_2(w, fine, s_g2, r_g2, sent)
    halo(sent)
    columns(sent)
    scatter_1(w, wpart, wgot1, s_w1, r_w1, sent)
    mix(sent)
    halo_back(sent)
    scatter_1(w, fpart, fgot1, s_f1, r_f1, sent)
    scatter_2(w, wrows, wgot2, s_w2, r_w2, sent)
    scatter_2(w, frows, fgot2, s_f2, r_f2, sent)
    gather_1(w, wfull, s_w3, r_w3, sent)
    gather_2(w, wfull, s_w4, r_w4, sent)


def shards(n, tps, queries, keys, values, out_weight, out_grad, near_offsets, coupling):
    tiles = 2 * n * n
    group = min(16, tiles)
    pieces = (tiles, SUB, LANE)
    dma = lambda *shape: pltpu.SemaphoreType.DMA(shape)
    vm = lambda dtype, *shape: pltpu.VMEM(shape, dtype)
    pair = [dma(2, n), dma(2, n)]
    in_vmem = pl.BlockSpec(memory_space=pltpu.VMEM)
    in_smem = pl.BlockSpec(memory_space=pltpu.SMEM)
    rest = FAR + tiles
    length = NEAR + rest
    sums = [vm(BF16, *pieces), vm(BF16, 2, n, n, SUB, LANE), vm(BF16, 2, n, SUB, LANE), vm(BF16, 2, n, SUB, LANE)]
    scratch = [
        vm(BF16, 2 * TOK, COLS), vm(BF16, 2 * TOK, COLS), vm(BF16, *pieces), vm(BF16, tps, TOK, COLS),
        vm(BF16, BLK, rest, COLS), vm(BF16, BLK, rest, COLS), vm(BF16, BLK * C1, tiles),
        vm(F32, BLK, length, COLS), vm(BF16, BLK, length, COLS), vm(BF16, TOK, COLS), vm(BF16, TOK, COLS), vm(F32, TOK, COLS),
        vm(BF16, tps, TOK, COLS), vm(BF16, tps, TOK, COLS), vm(F32, 2 * TOK, COLS), vm(F32, 2 * TOK, COLS),
        vm(BF16, 4, TOK // 2, COLS), vm(BF16, 4, TOK // 2, COLS), vm(BF16, BLK * C1, SUB * LANE), vm(F32, tiles, 2 * COLS),
        *sums, vm(BF16, *pieces), *sums,
        *pair, *pair, dma(4), dma(4), dma(tps), dma(tps), dma(tps), dma(tps), dma(4), dma(4),
        *pair, *pair, *pair, *pair, *pair, *pair,
    ]
    like = lambda x: jax.ShapeDtypeStruct(x.shape, BF16)
    return pl.pallas_call(
        functools.partial(kernel, n, tps, group),
        out_shape=(
            like(out_grad), like(queries), like(keys), like(values),
            jax.ShapeDtypeStruct(out_weight.shape, F32),
        ),
        in_specs=[in_smem] * 2 + [in_vmem] * 5,
        out_specs=[in_vmem] * 5,
        scratch_shapes=scratch,
        compiler_params=pltpu.CompilerParams(
            collective_id=0, has_side_effects=True, vmem_limit_bytes=48 * 1024 * 1024
        ),
    )(near_offsets, coupling, queries, keys, values, out_weight, out_grad)


def solution(mesh):
    n = int(round((mesh.shape["seq"] // 2) ** 0.5))
    step = functools.partial(shards, n, mesh.shape["tp"])
    in_specs = (
        P("seq", "tp"),
        P("seq", "tp"),
        P("seq", "tp"),
        P("tp", None),
        P("seq", "tp"),
        P("seq", None),
        P("seq", None),
    )
    out_specs = (P("seq", "tp"), P("seq", "tp"), P("seq", "tp"), P("seq", "tp"), P("tp", None))
    return jax.shard_map(step, mesh=mesh, in_specs=in_specs, out_specs=out_specs, check_vma=False)
```

time: 2140 us -> 77.9 us (0.04)
  waiting for transfers between devices: 1310 us -> 0 us
  blocking collectives: 720 us -> 0 us
  Pallas kernels: 0 us -> 67.4 us
  other arithmetic: 32 us -> 0 us
    unnamed x3 -> x0, waiting for transfers between devices: 1310 us -> none
    all_gather x3 -> x0, blocking collectives: 720 us -> none  [the longest x1 359 us: shards(): fine_all = lax.all_gather(fine_own, 'seq', axis=0, tiled=True)]
    pallas_call x0 -> x1, Pallas kernels: none -> 67.4 us  [shards(): pl.pallas_call(functools.partial(kernel, n, tps, group), out_shape=(like(...]
  transfers between devices with their start and end apart: 6 -> 0, of which waited for: 2 -> 0; matrix products, arithmetic and copies ran while one was open for 3% -> 0% of each run, Pallas kernels for 0% -> 0%
where the time goes in v1:
time: 77.9 us; the launch traced here: 77.6 us
  Pallas kernels  67.4 us (87%)
  local copies, waits for them, and re-layouts  9.6 us (12%)
    pallas_call x1, Pallas kernels, shards(): pl.pallas_call(functools.partial(kernel, n, tps, group), out_shape=(like(...  67.4 us
    unnamed x19, local copies, waits for them, and re-layouts  9.6 us

profile of v1, /device:TPU:6, one launch (start us, length us, event | category | flops | bytes accessed | tf_op | source)
XLA Modules:
  0.0 77.6 jit_solution(11155093225129608632)
XLA Ops:
  0.6 0.0 copy-start
  0.6 1.0 %copy-done = bf16[256,1024]{1,0:T(8,128)(2,1)S(1)} copy-done((bf16[256,1024]{1,0:T(8,128)(2,1)S(1)}, bf16[256,1024]{1,0:T(8,128)(2,1)}, u32[]{:S(2)}) %copy-start) | copy-done | bytes 524312
  1.7 0.0 copy-start.1
  1.7 0.9 %copy-done.1 = bf16[256,256]{1,0:T(8,128)(2,1)S(1)} copy-done((bf16[256,256]{1,0:T(8,128)(2,1)S(1)}, bf16[256,256]{1,0:T(8,128)(2,1)}, u32[]{:S(2)}) %copy-start.1) | copy-done | bytes 131096
  2.6 0.0 copy-start.2
  2.6 0.9 %copy-done.2 = bf16[256,256]{1,0:T(8,128)(2,1)S(1)} copy-done((bf16[256,256]{1,0:T(8,128)(2,1)S(1)}, bf16[256,256]{1,0:T(8,128)(2,1)}, u32[]{:S(2)}) %copy-start.2) | copy-done | bytes 131096
  3.5 0.0 copy-start.3
  3.5 0.9 %copy-done.3 = bf16[256,256]{1,0:T(8,128)(2,1)S(1)} copy-done((bf16[256,256]{1,0:T(8,128)(2,1)S(1)}, bf16[256,256]{1,0:T(8,128)(2,1)}, u32[]{:S(2)}) %copy-start.3) | copy-done | bytes 131096
  4.4 0.0 copy-start.4
  4.4 0.9 %copy-done.4 = bf16[256,256]{1,0:T(8,128)(2,1)S(1)} copy-done((bf16[256,256]{1,0:T(8,128)(2,1)S(1)}, bf16[256,256]{1,0:T(8,128)(2,1)}, u32[]{:S(2)}) %copy-start.4) | copy-done | bytes 131096
  5.3 0.0 copy-start.5
  5.3 0.7 copy-done.5
  6.0 0.0 copy-start.6
  6.0 0.7 copy-done.6
  6.7 67.4 %shard_map.110 = (bf16[256,256]{1,0:T(8,128)(2,1)S(1)}, bf16[256,256]{1,0:T(8,128)(2,1)S(1)}, bf16[256,256]{1,0:T(8,128)(2,1)S(1)}, bf16[256,256]{1,0:T(8,128)(2,1)S(1)}, f32[256,1024]{1,0:T(8,128)S(1)}) custom-call(s32[4,3]{1,0:T(4,128)S(1)} %copy-done.5, s32[4,16]{1,0:T(4,128)S(1)} %copy-done.6, bf16[256,256]{1,0:T(8,128)(2,1)S(1)} %copy-done.1, ...), custom_call_target="tpu_custom_call" | custom-call | tf_op jit(solution)/shard_map/pallas_call | solution.py:484
  74.1 0.7 copy.17
  74.7 0.7 copy.18
  75.4 0.7 copy.19
  76.0 0.7 copy.20
  76.7 1.0 %copy.21 = f32[256,1024]{1,0:T(8,128)} copy(f32[256,1024]{1,0:T(8,128)S(1)} %get-tuple-element.14) | data formatting | bytes 2097152
Async XLA Ops:
  0.6 1.0 %copy-start = (bf16[256,1024]{1,0:T(8,128)(2,1)S(1)}, bf16[256,1024]{1,0:T(8,128)(2,1)}, u32[]{:S(2)}) copy-start(bf16[256,1024]{1,0:T(8,128)(2,1)} %w_ref.1) | copy-start | bytes 1572868
  1.7 0.9 %copy-start.1 = (bf16[256,256]{1,0:T(8,128)(2,1)S(1)}, bf16[256,256]{1,0:T(8,128)(2,1)}, u32[]{:S(2)}) copy-start(bf16[256,256]{1,0:T(8,128)(2,1)} %q_ref.1) | copy-start | bytes 393220
  2.6 0.9 %copy-start.2 = (bf16[256,256]{1,0:T(8,128)(2,1)S(1)}, bf16[256,256]{1,0:T(8,128)(2,1)}, u32[]{:S(2)}) copy-start(bf16[256,256]{1,0:T(8,128)(2,1)} %k_ref.1) | copy-start | bytes 393220
  3.5 0.9 %copy-start.3 = (bf16[256,256]{1,0:T(8,128)(2,1)S(1)}, bf16[256,256]{1,0:T(8,128)(2,1)}, u32[]{:S(2)}) copy-start(bf16[256,256]{1,0:T(8,128)(2,1)} %v_ref.1) | copy-start | bytes 393220
  4.4 0.9 %copy-start.4 = (bf16[256,256]{1,0:T(8,128)(2,1)S(1)}, bf16[256,256]{1,0:T(8,128)(2,1)}, u32[]{:S(2)}) copy-start(bf16[256,256]{1,0:T(8,128)(2,1)} %og_ref.1) | copy-start | bytes 393220
  5.3 0.7 copy-start.5
  6.0 0.7 copy-start.6

commit v2 on v1

v2 whole, which is shorter than its diff:
```python
import functools

import jax
import jax.numpy as jnp
from jax import lax
from jax.experimental import pallas as pl
from jax.experimental.pallas import tpu as pltpu
from jax.sharding import PartitionSpec as P

MESH = pl.DeviceIdType.MESH
F32 = jnp.float32
BF16 = jnp.bfloat16
HD = 64
NB = 64
BLK = 4
HEADS = 4
COLS = HEADS * HD
TOK = BLK * NB
C1 = 16
LANE = 128
SUB = 16
NEAR = 5 * NB
FAR = C1 * BLK
VMEM = 62 * 1024 * 1024


def each(low, high, body):
    lax.fori_loop(low, high, lambda k, c: (body(k), c)[1], 0)


def dot_nn(a, b):
    return lax.dot_general(a, b, (((1,), (0,)), ((), ())), preferred_element_type=F32)


def dot_nt(a, b):
    return lax.dot_general(a, b, (((1,), (1,)), ((), ())), preferred_element_type=F32)


def dot_tn(a, b):
    return lax.dot_general(a, b, (((0,), (0,)), ((), ())), preferred_element_type=F32)


def iota(shape, dim):
    return lax.broadcasted_iota(jnp.int32, shape, dim)


class Place:
    def __init__(self, n, tps):
        self.n, self.tps = n, tps
        self.seqs = 2 * n * n
        self.seq = lax.axis_index("seq")
        self.tp = lax.axis_index("tp")
        self.z = lax.div(self.seq, 2 * n)
        self.y = lax.rem(lax.div(self.seq, 2), n)
        self.xh = lax.rem(self.seq, 2)
        self.mine = self.z * (1 - self.xh) + self.y * self.xh
        self.cross = self.y * (1 - self.xh) + self.z * self.xh

    def by(self, slot):
        odd = lax.rem(slot, 2)
        return odd * lax.div(slot + 1, 2) + (1 - odd) * (self.n - lax.div(slot, 2))

    def back(self, slot):
        return slot + 2 * lax.rem(slot, 2) - 1 - lax.div(slot, self.n - 1)

    def slot(self, ahead):
        n = self.n
        upper = lax.div(n - 1 + n // 2 - ahead, n - 1)
        return upper * (2 * ahead - 1) + (1 - upper) * 2 * (n - ahead) + lax.div(n - 1 - ahead, n - 1)

    def at(self, z, y, xh):
        return (z * (2 * self.n) + y * 2 + xh, self.tp)

    def along_mine(self, slot, xh):
        c = lax.rem(self.mine + self.by(slot), self.n)
        return self.at(c * (1 - self.xh) + self.z * self.xh, self.y * (1 - self.xh) + c * self.xh, xh)

    def along_cross(self, slot, xh):
        c = lax.rem(self.cross + self.by(slot), self.n)
        return self.at(self.z * (1 - self.xh) + c * self.xh, c * (1 - self.xh) + self.y * self.xh, xh)

    def along_y(self, slot):
        return self.at(self.z, lax.rem(self.y + self.by(slot), self.n), self.xh)

    def along_z(self, slot):
        return self.at(lax.rem(self.z + self.by(slot), self.n), self.y, self.xh)

    def step(self, by):
        return (lax.rem(self.seq + self.seqs + by, self.seqs), self.tp)

    def tp_at(self, k):
        c = lax.rem(self.tp + k, self.tps)
        return c, (self.seq, c)

    def spots(self):
        n = self.n
        of_y = [self.slot(lax.rem(c + n - self.y, n)) for c in range(n)]
        of_z = [self.slot(lax.rem(c + n - self.z, n)) for c in range(n)]
        return [
            h * n * n + (of_z if h else of_y)[r] * n + (of_y if h else of_z)[c]
            for h in range(2)
            for r in range(n)
            for c in range(n)
        ]


def remote(src, dst, send, recv, device):
    return pltpu.make_async_remote_copy(
        src_ref=src, dst_ref=dst, send_sem=send, recv_sem=recv, device_id=device, device_id_type=MESH
    )


class Flight:
    def __init__(self, log, move, *args):
        self.move, self.args = move, args
        log.append(self)

    def begin(self):
        self.move(*self.args, lambda copy: copy.start())

    def land(self):
        self.move(*self.args, lambda copy: copy.wait_recv())

    def end(self):
        self.move(*self.args, lambda copy: copy.wait_send())


def spread(w, buf, send, recv, other, low, high, act):
    own = buf.at[w.xh * w.n * w.n]

    def one(i):
        into = buf.at[w.xh * w.n * w.n + w.back(i)]
        xh = 1 - w.xh if other else w.xh
        act(remote(own, into, send.at[other, i], recv.at[other, w.back(i)], w.along_mine(i, xh)))

    if low == 0:
        if other:
            act(remote(own, own, send.at[1, 0], recv.at[1, 0], w.at(w.z, w.y, 1 - w.xh)))
        low = 1
    each(low, high, one)


def relay(w, buf, send, recv, batch, other, low, high, act):
    n = w.n
    base = (1 - w.xh if other else w.xh) * n * n

    def one(i):
        j = w.back(i)
        mine = buf.at[pl.ds(base + low, high - low)]
        into = buf.at[pl.ds(base + j * n + low, high - low)]
        device = (w.along_mine if other else w.along_cross)(i, w.xh)
        act(remote(mine, into, send.at[batch, i], recv.at[batch, j], device))

    each(1, n, one)


class Gather:
    def __init__(self, log, w, buf, s_1, r_1, s_2, r_2):
        n = w.n
        cuts = [c for c in (1, 3, 5, 8) if c < n] + [n]
        same = list(zip([0] + cuts[:-1], cuts))
        cross = [(0, cuts[1])] + same[2:]
        self.out = [Flight(log, spread, w, buf, s_1, r_1, 1, 0, n), Flight(log, spread, w, buf, s_1, r_1, 0, 0, n)]
        steps = [(0, *part) for part in same] + [(1, *part) for part in cross]
        steps.sort(key=lambda step: (step[1] + 2 * step[0], step[0]))
        self.arrive = [Flight([], spread, w, buf, s_1, r_1, *step) for step in steps]
        self.onward = [Flight(log, relay, w, buf, s_2, r_2, i, *step) for i, step in enumerate(steps)]

    def begin(self):
        self.out[1].begin()
        self.out[0].begin()
        self.onward[0].begin()

    def forward(self):
        for arrived, onward in zip(self.arrive[1:], self.onward[1:]):
            arrived.land()
            onward.begin()

    def land(self):
        for onward in self.onward:
            onward.land()


def to_rows(w, part, got, send, recv, batch, low, high, act):
    n = w.n

    def one(i):
        for h, device in ((0, w.along_y(i)), (1, w.along_z(i))):
            mine = part.at[pl.ds(h * n * n + i * n + low, high - low)]
            act(remote(mine, got.at[h, i, pl.ds(low, high - low)], send.at[batch, h, i], recv.at[batch, h, i], device))

    each(1, n, one)


def to_owners(w, rows, got, send, recv, low, high, act):
    def same(i):
        act(remote(rows.at[w.xh, i], got.at[0, i], send.at[0, i], recv.at[0, i], w.along_mine(i, w.xh)))

    def other(i):
        act(remote(rows.at[1 - w.xh, i], got.at[1, i], send.at[1, i], recv.at[1, i], w.along_cross(i, 1 - w.xh)))

    each(max(low, 1), high, same)
    if low == 0:
        act(remote(rows.at[1 - w.xh, 0], got.at[1, 0], send.at[1, 0], recv.at[1, 0], w.at(w.z, w.y, 1 - w.xh)))
    each(max(low, 1), high, other)


class Scatter:
    def __init__(self, log, w, part, got_1, rows, got_2, s_1, r_1, s_2, r_2, cut):
        n = w.n
        self.w, self.part, self.got_1, self.rows, self.got_2 = w, part, got_1, rows, got_2
        self.cols = [(cut, n), (0, cut)] if cut else [(0, n)]
        self.first = [Flight(log, to_rows, w, part, got_1, s_1, r_1, i, *c) for i, c in enumerate(self.cols)]
        self.second = [Flight(log, to_owners, w, rows, got_2, s_2, r_2, *c) for c in self.cols]

    def begin(self):
        for first in self.first:
            first.begin()

    def forward(self):
        n = self.w.n
        for (low, high), first, second in zip(self.cols, self.first, self.second):
            first.land()
            for h in range(2):
                total = self.part[h * n * n + low : h * n * n + high].astype(F32)
                for i in range(1, n):
                    total += self.got_1[h, i, low:high].astype(F32)
                self.rows[h, low:high] = total.astype(BF16)
            second.begin()

    def land(self):
        for second in self.second:
            second.land()
        total = self.rows[self.w.xh, 0].astype(F32)
        for i in range(1, self.w.n):
            total += self.got_2[0, i].astype(F32)
        for i in range(self.w.n):
            total += self.got_2[1, i].astype(F32)
        return total


def kernel(
    n, tps, group,
    off_in, cpl_in, q_in, k_in, v_in, w_in, og_in,
    mixed_out, gq_out, gk_out, gv_out, pieces_out,
    off_ref, cpl_ref, q_ref, k_ref, v_ref, w_ref, og_ref, s_in,
    mixed_ref, gq_ref, gk_ref, gv_ref, s_out,
    kpad, vpad, fine, ogs, kft, vft, hot, probs, halves, att, gatt, mine_out,
    msend, mgot, gkpad, gvpad, hsend, hgot, dlist, dtop,
    wpart, wgot1, wrows, wgot2, wfull, fpart, fgot1, frows, fgot2,
    s_h, r_h, s_o, r_o, s_m, r_m, s_b, r_b,
    s_g1, r_g1, s_g2, r_g2, s_w1, r_w1, s_w2, r_w2, s_w3, r_w3, s_w4, r_w4, s_f1, r_f1, s_f2, r_f2,
):
    w = Place(n, tps)
    tiles = w.seqs
    groups = tiles // group
    nblk = tiles * BLK
    half = TOK // 2
    flights = []

    brought = [
        pltpu.make_async_copy(src, dst, s_in.at[i])
        for i, (src, dst) in enumerate(
            ((k_in, k_ref), (v_in, v_ref), (og_in, og_ref), (cpl_in, cpl_ref), (off_in, off_ref), (q_in, q_ref), (w_in, w_ref))
        )
    ]
    for copy in brought:
        copy.start()

    barrier = pltpu.get_barrier_semaphore()

    def greet(device):
        pl.semaphore_signal(barrier, inc=1, device_id=device, device_id_type=MESH)

    def greet_square(i):
        greet(w.along_y(i))
        greet(w.along_z(i))
        greet(w.along_mine(i, 1 - w.xh))
        greet(w.along_cross(i, 1 - w.xh))

    each(1, n, greet_square)
    greet(w.at(w.z, w.y, 1 - w.xh))
    greet(w.step(1))
    greet(w.step(-1))
    each(1, tps, lambda k: greet(w.tp_at(k)[1]))

    for copy in brought[:2]:
        copy.wait()
    piece = jnp.zeros((SUB, LANE), F32)
    for c in range(4):
        row, tok = iota((SUB, TOK), 0), iota((SUB, TOK), 1)
        pick = jnp.where((row - c * BLK) == (tok >> 6), 1.0, 0.0).astype(BF16)
        src = k_ref if c < 2 else v_ref
        piece += dot_nn(pick, src[:, (c % 2) * LANE : (c % 2 + 1) * LANE])
    fine[w.xh * n * n] = (piece * 0.125).astype(BF16)
    pl.semaphore_wait(barrier, 4 * (n - 1) + 3 + tps - 1)

    def move_halo(act):
        for i, (src, pad) in enumerate(((k_ref, kpad), (v_ref, vpad))):
            act(remote(src.at[pl.ds(half, half)], pad.at[pl.ds(0, half)], s_h.at[i], r_h.at[i], w.step(1)))
            act(remote(src.at[pl.ds(0, half)], pad.at[pl.ds(half + TOK, half)], s_h.at[2 + i], r_h.at[2 + i], w.step(-1)))

    def move_columns(act):
        def one(k):
            act(remote(og_ref, ogs.at[w.tp], s_o.at[k], r_o.at[k], w.tp_at(k)[1]))

        each(1, tps, one)

    summaries = Gather(flights, w, fine, s_g1, r_g1, s_g2, r_g2)
    halo = Flight(flights, move_halo)
    columns = Flight(flights, move_columns)
    summaries.begin()
    halo.begin()
    brought[2].wait()
    columns.begin()

    ogs[w.tp] = og_ref[...]
    kpad[half : half + TOK] = k_ref[...]
    vpad[half : half + TOK] = v_ref[...]
    gkpad[...] = jnp.zeros_like(gkpad)
    gvpad[...] = jnp.zeros_like(gvpad)
    dtop[...] = jnp.zeros_like(dtop)
    for copy in brought[3:]:
        copy.wait()

    bits = n.bit_length() - 1
    place = iota((1, tiles), 1)

    def ahead(slot):
        return jnp.where((slot & 1) == 1, (slot + 1) >> 1, n - (slot >> 1))

    by_row, by_col = ahead((place >> bits) & (n - 1)), ahead(place & (n - 1))
    tile_of = jnp.where(
        place < n * n,
        ((w.z + by_col) & (n - 1)) * (2 * n) + ((w.y + by_row) & (n - 1)) * 2,
        ((w.z + by_row) & (n - 1)) * (2 * n) + ((w.y + by_col) & (n - 1)) * 2 + 1,
    )
    rows8 = iota((8, tiles), 0)
    listed = []
    for g in range(BLK * C1 // 8):
        wanted = jnp.zeros((8, tiles), jnp.int32)
        for i in range(8):
            at = g * 8 + i
            wanted = jnp.where(rows8 == i, cpl_ref[at // C1, at % C1], wanted)
        listed.append(wanted)
    wanted = jnp.concatenate(listed, 0)
    hot[...] = jnp.where(wanted == tile_of, 1.0, 0.0).astype(BF16)

    size = group * SUB
    to, fro = iota((size, size), 0), iota((size, size), 1)
    gbits = group.bit_length() - 1
    swapped = (fro & (SUB - 1)) * group + (fro >> 4)
    swap = jnp.where(to == swapped, 1.0, 0.0).astype(BF16)
    swapped = (fro & (group - 1)) * SUB + (fro >> gbits)
    swap_back = jnp.where(to == swapped, 1.0, 0.0).astype(BF16)

    head_of = iota((1, COLS), 1) >> 6
    masks = [jnp.where(head_of == h, 1.0, 0.0) for h in range(HEADS)]
    masks_b = [m.astype(BF16) for m in masks]

    def diagonal(rows):
        return jnp.concatenate([rows * m for m in masks_b], 0)

    def collect(full):
        out = full[0:NB] * masks[0]
        for h in range(1, HEADS):
            out += full[h * NB : (h + 1) * NB] * masks[h]
        return out

    summaries.forward()

    columns.land()
    grad = dot_nt(ogs[0], w_ref[:, 0:COLS])
    for t in range(1, tps):
        grad += dot_nt(ogs[t], w_ref[:, t * COLS : (t + 1) * COLS])
    gatt[...] = grad.astype(BF16)
    spots = w.spots()

    halo.land()
    summaries.land()

    packed = jnp.concatenate([fine[g * group : (g + 1) * group].reshape(size, LANE) for g in range(groups)], 1)
    by_row = dot_nn(swap, packed)
    flat = jnp.concatenate(
        [
            jnp.concatenate([by_row[s * group : (s + 1) * group, g * LANE : (g + 1) * LANE] for s in range(SUB)], 1)
            for g in range(groups)
        ],
        0,
    )
    tops = []
    for c in range(4):
        total = flat[:, c * BLK * LANE : (c * BLK + 1) * LANE]
        for r in range(1, BLK):
            total += flat[:, (c * BLK + r) * LANE : (c * BLK + r + 1) * LANE]
        tops.append((total * 0.5).astype(BF16))
    far = dot_nn(hot[...], flat.astype(BF16)).astype(BF16)
    for b in range(BLK):
        for r in range(BLK):
            for c in range(4):
                s = c * BLK + r
                into = kft if c < 2 else vft
                into[b, r * C1 : (r + 1) * C1, (c % 2) * LANE : (c % 2 + 1) * LANE] = far[
                    b * C1 : (b + 1) * C1, s * LANE : (s + 1) * LANE
                ]
        kft[b, FAR:, :LANE], kft[b, FAR:, LANE:] = tops[0], tops[1]
        vft[b, FAR:, :LANE], vft[b, FAR:, LANE:] = tops[2], tops[3]

    def listed_rows(pad, rest, b):
        return jnp.concatenate([pad[b * NB : b * NB + NEAR], rest[b]], 0)

    for b in range(BLK):
        keys = listed_rows(kpad, kft, b)
        vals = listed_rows(vpad, vft, b)
        scores = dot_nt(keys, diagonal(q_ref[b * NB : (b + 1) * NB])) * 0.125
        parts = []
        for d in range(5):
            target = w.seq * BLK + b + d - 2
            chosen = (off_ref[b, 0] == d - 2) | (off_ref[b, 1] == d - 2) | (off_ref[b, 2] == d - 2)
            usable = chosen & (target >= 0) & (target < nblk)
            parts.append(scores[d * NB : (d + 1) * NB] + jnp.where(usable, 0.0, -1e30))
        scores = jnp.concatenate(parts + [scores[NEAR:]], 0)
        peak = jnp.max(scores, 0, keepdims=True)
        exps = jnp.exp(scores - peak)
        prob = exps * (1.0 / jnp.sum(exps, 0, keepdims=True))
        prob_b = prob.astype(BF16)
        probs[b] = prob
        halves[b] = prob_b
        att[b * NB : (b + 1) * NB] = collect(dot_tn(prob_b, vals)).astype(BF16)

    for t in range(tps):
        part = dot_tn(att[...], ogs[t]).astype(BF16)
        for j in range(COLS // LANE):
            for i in range(TOK // SUB):
                wpart[spots[(t * 2 + j) * 16 + i]] = part[i * SUB : (i + 1) * SUB, j * LANE : (j + 1) * LANE]
    weight = Scatter(flights, w, wpart, wgot1, wrows, wgot2, s_w1, r_w1, s_w2, r_w2, 5 if n == 8 else n - 1)
    whole = Gather(flights, w, wfull, s_w3, r_w3, s_w4, r_w4)
    weight.begin()

    for t in range(tps):
        msend[t] = dot_nn(att[...], w_ref[:, t * COLS : (t + 1) * COLS]).astype(BF16)

    def move_mix(act):
        def one(k):
            c, device = w.tp_at(k)
            act(remote(msend.at[c], mgot.at[k], s_m.at[k], r_m.at[k], device))

        each(1, tps, one)

    mix = Flight(flights, move_mix)
    mix.begin()
    mine_out[...] = dot_nn(att[...], w_ref[:, pl.ds(pl.multiple_of(w.tp * COLS, COLS), COLS)])

    for b in range(BLK):
        keys = listed_rows(kpad, kft, b)
        vals = listed_rows(vpad, vft, b)
        q_diag = diagonal(q_ref[b * NB : (b + 1) * NB])
        g_diag = diagonal(gatt[b * NB : (b + 1) * NB])
        prob = probs[b]
        dprob = dot_nt(vals, g_diag)
        inner = jnp.sum(prob * dprob, 0, keepdims=True)
        dscore = (prob * (dprob - inner) * 0.125).astype(BF16)
        gq_ref[b * NB : (b + 1) * NB] = collect(dot_tn(dscore, keys)).astype(BF16)
        dkey = dot_nn(dscore, q_diag)
        dval = dot_nn(halves[b], g_diag)
        gkpad[b * NB : b * NB + NEAR] += dkey[:NEAR]
        gvpad[b * NB : b * NB + NEAR] += dval[:NEAR]
        for r in range(BLK):
            for c in range(4):
                s = c * BLK + r
                src = dkey if c < 2 else dval
                dlist[b * C1 : (b + 1) * C1, s * LANE : (s + 1) * LANE] = src[
                    NEAR + r * C1 : NEAR + (r + 1) * C1, (c % 2) * LANE : (c % 2 + 1) * LANE
                ].astype(BF16)
        dtop[:, :COLS] += dkey[NEAR + FAR :]
        dtop[:, COLS:] += dval[NEAR + FAR :]

    for i, pad in enumerate((gkpad, gvpad)):
        hsend[i] = pad[half + TOK :].astype(BF16)
        hsend[2 + i] = pad[:half].astype(BF16)

    def move_back(act):
        for i in range(2):
            act(remote(hsend.at[i], hgot.at[i], s_b.at[i], r_b.at[i], w.step(1)))
            act(remote(hsend.at[2 + i], hgot.at[2 + i], s_b.at[2 + i], r_b.at[2 + i], w.step(-1)))

    tile_grad = dot_tn(hot[...], dlist[...])
    cols = []
    for c in range(4):
        for r in range(BLK):
            s = c * BLK + r
            cols.append(tile_grad[:, s * LANE : (s + 1) * LANE] + dtop[:, c * LANE : (c + 1) * LANE] * 0.5)
    by_row = jnp.concatenate(
        [
            jnp.concatenate([cols[s][g * group : (g + 1) * group] for s in range(SUB)], 0)
            for g in range(groups)
        ],
        1,
    ).astype(BF16)
    packed = dot_nn(swap_back, by_row).astype(BF16)
    for g in range(groups):
        fpart[g * group : (g + 1) * group] = packed[:, g * LANE : (g + 1) * LANE].reshape(group, SUB, LANE)
    halo_back = Flight(flights, move_back)
    halo_back.begin()
    coupled = Scatter(flights, w, fpart, fgot1, frows, fgot2, s_f1, r_f1, s_f2, r_f2, 0)
    coupled.begin()

    weight.forward()

    mix.land()
    total = mine_out[...]
    for k in range(1, tps):
        total += mgot[k].astype(F32)
    mixed_ref[...] = total.astype(BF16)
    taken = [
        pltpu.make_async_copy(src, dst, s_out.at[i])
        for i, (src, dst) in enumerate(
            ((mixed_ref, mixed_out), (gq_ref, gq_out), (gk_ref, gk_out), (gv_ref, gv_out), (wfull, pieces_out))
        )
    ]
    for copy in taken[:2]:
        copy.start()
    halo_back.land()

    wfull[w.xh * n * n] = weight.land().astype(BF16)
    whole.begin()
    coupled.forward()
    whole.forward()

    fine_grad = coupled.land() * 0.125
    for i, (pad, out) in enumerate(((gkpad, gk_ref), (gvpad, gv_ref))):
        for r in range(BLK):
            rows = pad[half + r * NB : half + (r + 1) * NB]
            if r < BLK // 2:
                rows += hgot[i, r * NB : (r + 1) * NB].astype(F32)
            else:
                rows += hgot[2 + i, r * NB - half : (r + 1) * NB - half].astype(F32)
            for c in range(2):
                s = (2 * i + c) * BLK + r
                out[r * NB : (r + 1) * NB, c * LANE : (c + 1) * LANE] = (
                    rows[:, c * LANE : (c + 1) * LANE] + fine_grad[s : s + 1]
                ).astype(BF16)
    for copy in taken[2:4]:
        copy.start()

    whole.land()
    taken[4].start()
    for flight in flights:
        flight.end()
    for copy in taken:
        copy.wait()


def hand_over(n, tps, *refs):
    given, made, held, pieces, weight, sems_in, sems_out = refs[:5], refs[5:10], refs[10:14], *refs[14:]
    into = [pltpu.make_async_copy(src, dst, sems_in.at[i]) for i, (src, dst) in enumerate(zip(given, (*held, pieces)))]
    for i in (4, 0, 1, 2, 3):
        into[i].start()
    out = [pltpu.make_async_copy(src, dst, sems_out.at[i]) for i, (src, dst) in enumerate(zip(held, made))]
    spots = Place(n, tps).spots()
    into[4].wait()
    for j in range(tps * COLS // LANE):
        cols = pl.ds(j * LANE, LANE)
        for i in range(TOK // SUB):
            weight[i * SUB : (i + 1) * SUB, cols] = pieces[spots[j * 16 + i]].astype(F32)
        out.append(pltpu.make_async_copy(weight.at[:, cols], made[4].at[:, cols], sems_out.at[4 + j]))
        out[-1].start()
        if j < 4:
            into[j].wait()
            out[j].start()
    for j in range(tps * COLS // LANE, 4):
        into[j].wait()
        out[j].start()
    for copy in out:
        copy.wait()


def shards(n, tps, queries, keys, values, out_weight, out_grad, near_offsets, coupling):
    tiles = 2 * n * n
    group = min(16, tiles)
    pieces = (tiles, SUB, LANE)
    dma = lambda *shape: pltpu.SemaphoreType.DMA(shape)
    vm = lambda dtype, *shape: pltpu.VMEM(shape, dtype)
    pair = [dma(2, n)] * 2
    relays = [dma(8, n)] * 2
    rowwise = [dma(2, 2, n)] * 2
    keep = [vm(BF16, TOK, COLS)] * 4
    in_place = pl.BlockSpec(memory_space=pltpu.HBM)
    rest = FAR + tiles
    length = NEAR + rest
    sums = [vm(BF16, *pieces), vm(BF16, 2, n, n, SUB, LANE), vm(BF16, 2, n, SUB, LANE), vm(BF16, 2, n, SUB, LANE)]
    scratch = [
        pltpu.SMEM(near_offsets.shape, jnp.int32), pltpu.SMEM(coupling.shape, jnp.int32),
        *(vm(BF16, *x.shape) for x in (queries, keys, values, out_weight, out_grad)), dma(7),
        *keep, dma(5),
        vm(BF16, 2 * TOK, COLS), vm(BF16, 2 * TOK, COLS), vm(BF16, *pieces), vm(BF16, tps, TOK, COLS),
        vm(BF16, BLK, rest, COLS), vm(BF16, BLK, rest, COLS), vm(BF16, BLK * C1, tiles),
        vm(F32, BLK, length, COLS), vm(BF16, BLK, length, COLS), vm(BF16, TOK, COLS), vm(BF16, TOK, COLS), vm(F32, TOK, COLS),
        vm(BF16, tps, TOK, COLS), vm(BF16, tps, TOK, COLS), vm(F32, 2 * TOK, COLS), vm(F32, 2 * TOK, COLS),
        vm(BF16, 4, TOK // 2, COLS), vm(BF16, 4, TOK // 2, COLS), vm(BF16, BLK * C1, SUB * LANE), vm(F32, tiles, 2 * COLS),
        *sums, vm(BF16, *pieces), *sums,
        dma(4), dma(4), dma(tps), dma(tps), dma(tps), dma(tps), dma(4), dma(4),
        *pair, *relays, *rowwise, *pair, *pair, *relays, *rowwise, *pair,
    ]
    like = lambda x: jax.ShapeDtypeStruct(x.shape, BF16)
    shapes = (like(out_grad), like(queries), like(keys), like(values))
    weight_grad = jax.ShapeDtypeStruct(out_weight.shape, F32)
    results = pl.pallas_call(
        functools.partial(kernel, n, tps, group),
        out_shape=(*shapes, jax.ShapeDtypeStruct(pieces, BF16)),
        in_specs=[in_place] * 7,
        out_specs=[in_place] * 5,
        scratch_shapes=scratch,
        compiler_params=pltpu.CompilerParams(collective_id=0, has_side_effects=True, vmem_limit_bytes=VMEM),
    )(near_offsets, coupling, queries, keys, values, out_weight, out_grad)
    return pl.pallas_call(
        functools.partial(hand_over, n, tps),
        out_shape=(*shapes, weight_grad),
        in_specs=[in_place] * 5,
        out_specs=[in_place] * 5,
        scratch_shapes=[*keep, vm(BF16, *pieces), vm(F32, *out_weight.shape), dma(5), dma(4 + tps * COLS // LANE)],
        compiler_params=pltpu.CompilerParams(vmem_limit_bytes=VMEM),
    )(*results)


def solution(mesh):
    n = int(round((mesh.shape["seq"] // 2) ** 0.5))
    step = functools.partial(shards, n, mesh.shape["tp"])
    in_specs = (
        P("seq", "tp"),
        P("seq", "tp"),
        P("seq", "tp"),
        P("tp", None),
        P("seq", "tp"),
        P("seq", None),
        P("seq", None),
    )
    out_specs = (P("seq", "tp"), P("seq", "tp"), P("seq", "tp"), P("seq", "tp"), P("tp", None))
    return jax.shard_map(step, mesh=mesh, in_specs=in_specs, out_specs=out_specs, check_vma=False)
```

time: 77.9 us -> 71.9 us (0.923); the launches traced: 77.6 us -> 70.6 us
  local copies, waits for them, and re-layouts: 9.6 us -> 0 us
  Pallas kernels: 67.4 us -> 70 us
    unnamed x19 -> x0, local copies, waits for them, and re-layouts: 9.6 us -> none
    pallas_call x1 -> x2, Pallas kernels: 67.4 us -> 70 us  [the longest x1 67.6 us: shards(): pl.pallas_call(functools.partial(kernel, n, tps, group), out_shape=(*shap...]
where the time goes in v2:
time: 71.9 us; the launch traced here: 70.6 us
  Pallas kernels  70 us (97%)
    pallas_call x1, Pallas kernels, shards(): pl.pallas_call(functools.partial(kernel, n, tps, group), out_shape=(*shap...  67.6 us
    pallas_call x1, Pallas kernels, shards(): pl.pallas_call(functools.partial(hand_over, n, tps), out_shape=(*shapes,...  2.34 us

profile of v2, /device:TPU:6, one launch (start us, length us, event | category | flops | bytes accessed | tf_op | source)
XLA Modules:
  0.0 70.6 jit_solution(13491222228899159051)
XLA Ops:
  0.6 67.6 %shard_map.110 = (bf16[256,256]{1,0:T(8,128)(2,1)}, bf16[256,256]{1,0:T(8,128)(2,1)}, bf16[256,256]{1,0:T(8,128)(2,1)}, bf16[256,256]{1,0:T(8,128)(2,1)}, bf16[128,16,128]{2,1,0:T(8,128)(2,1)}) custom-call(s32[4,3]{1,0:T(4,128)} %off_in.1, s32[4,16]{1,0:T(4,128)} %cpl_in.1, bf16[256,256]{1,0:T(8,128)(2,1)} %q_in.1, bf16[256,256]{1,0:T(8,128)(2,1)} %k_in.1, ...), custom_call_target="tpu_custom_call" | custom-call | tf_op jit(solution)/shard_map/pallas_call | solution.py:608
  68.3 2.3 %shard_map.111 = (bf16[256,256]{1,0:T(8,128)(2,1)}, bf16[256,256]{1,0:T(8,128)(2,1)}, bf16[256,256]{1,0:T(8,128)(2,1)}, bf16[256,256]{1,0:T(8,128)(2,1)}, f32[256,1024]{1,0:T(8,128)}) custom-call(bf16[256,256]{1,0:T(8,128)(2,1)} %get-tuple-element.10.refs_0_, bf16[256,256]{1,0:T(8,128)(2,1)} %get-tuple-element.11.refs_1_, ...), custom_call_target="tpu_custom_call" | custom-call | tf_op jit(solution)/shard_map/pallas_call | solution.py:616

commit v3 on v2

--- a/solution.py
+++ b/solution.py
@@ -21,11 +21,11 @@
 SUB = 16
 NEAR = 5 * NB
 FAR = C1 * BLK
-VMEM = 62 * 1024 * 1024
+VMEM = 48 * 1024 * 1024
 
 
 def each(low, high, body):
-    lax.fori_loop(low, high, lambda k, c: (body(k), c)[1], 0)
+    lax.fori_loop(low, high, lambda k, c: (body(low + high - 1 - k), c)[1], 0)
 
 
 def dot_nn(a, b):
@@ -242,9 +242,8 @@
 def kernel(
     n, tps, group,
     off_in, cpl_in, q_in, k_in, v_in, w_in, og_in,
-    mixed_out, gq_out, gk_out, gv_out, pieces_out,
+    mixed_ref, gq_ref, gk_ref, gv_ref, pieces_ref,
     off_ref, cpl_ref, q_ref, k_ref, v_ref, w_ref, og_ref, s_in,
-    mixed_ref, gq_ref, gk_ref, gv_ref, s_out,
     kpad, vpad, fine, ogs, kft, vft, hot, probs, halves, att, gatt, mine_out,
     msend, mgot, gkpad, gvpad, hsend, hgot, dlist, dtop,
     wpart, wgot1, wrows, wgot2, wfull, fpart, fgot1, frows, fgot2,
@@ -369,13 +368,7 @@
 
     summaries.forward()
 
-    columns.land()
-    grad = dot_nt(ogs[0], w_ref[:, 0:COLS])
-    for t in range(1, tps):
-        grad += dot_nt(ogs[t], w_ref[:, t * COLS : (t + 1) * COLS])
-    gatt[...] = grad.astype(BF16)
     spots = w.spots()
-
     halo.land()
     summaries.land()
 
@@ -428,6 +421,7 @@
         halves[b] = prob_b
         att[b * NB : (b + 1) * NB] = collect(dot_tn(prob_b, vals)).astype(BF16)
 
+    columns.land()
     for t in range(tps):
         part = dot_tn(att[...], ogs[t]).astype(BF16)
         for j in range(COLS // LANE):
@@ -450,6 +444,11 @@
     mix = Flight(flights, move_mix)
     mix.begin()
     mine_out[...] = dot_nn(att[...], w_ref[:, pl.ds(pl.multiple_of(w.tp * COLS, COLS), COLS)])
+
+    grad = dot_nt(ogs[0], w_ref[:, 0:COLS])
+    for t in range(1, tps):
+        grad += dot_nt(ogs[t], w_ref[:, t * COLS : (t + 1) * COLS])
+    gatt[...] = grad.astype(BF16)
 
     for b in range(BLK):
         keys = listed_rows(kpad, kft, b)
@@ -503,23 +502,15 @@
     halo_back = Flight(flights, move_back)
     halo_back.begin()
     coupled = Scatter(flights, w, fpart, fgot1, frows, fgot2, s_f1, r_f1, s_f2, r_f2, 0)
+
+    weight.forward()
     coupled.begin()
-
-    weight.forward()
 
     mix.land()
     total = mine_out[...]
     for k in range(1, tps):
         total += mgot[k].astype(F32)
     mixed_ref[...] = total.astype(BF16)
-    taken = [
-        pltpu.make_async_copy(src, dst, s_out.at[i])
-        for i, (src, dst) in enumerate(
-            ((mixed_ref, mixed_out), (gq_ref, gq_out), (gk_ref, gk_out), (gv_ref, gv_out), (wfull, pieces_out))
-        )
-    ]
-    for copy in taken[:2]:
-        copy.start()
     halo_back.land()
 
     wfull[w.xh * n * n] = weight.land().astype(BF16)
@@ -540,37 +531,28 @@
                 out[r * NB : (r + 1) * NB, c * LANE : (c + 1) * LANE] = (
                     rows[:, c * LANE : (c + 1) * LANE] + fine_grad[s : s + 1]
                 ).astype(BF16)
-    for copy in taken[2:4]:
+
+    for flight in flights:
+        if flight not in whole.onward:
+            flight.end()
+    whole.land()
+    pieces_ref[...] = wfull[...]
+    for onward in whole.onward:
+        onward.end()
+
+
+def hand_over(n, tps, *refs):
+    held, pieces, made, weight, sems = refs[:4], refs[4], refs[5:10], *refs[10:]
+    out = [pltpu.make_async_copy(src, dst, sems.at[i]) for i, (src, dst) in enumerate(zip(held, made))]
+    for copy in out:
         copy.start()
-
-    whole.land()
-    taken[4].start()
-    for flight in flights:
-        flight.end()
-    for copy in taken:
-        copy.wait()
-
-
-def hand_over(n, tps, *refs):
-    given, made, held, pieces, weight, sems_in, sems_out = refs[:5], refs[5:10], refs[10:14], *refs[14:]
-    into = [pltpu.make_async_copy(src, dst, sems_in.at[i]) for i, (src, dst) in enumerate(zip(given, (*held, pieces)))]
-    for i in (4, 0, 1, 2, 3):
-        into[i].start()
-    out = [pltpu.make_async_copy(src, dst, sems_out.at[i]) for i, (src, dst) in enumerate(zip(held, made))]
     spots = Place(n, tps).spots()
-    into[4].wait()
     for j in range(tps * COLS // LANE):
         cols = pl.ds(j * LANE, LANE)
         for i in range(TOK // SUB):
             weight[i * SUB : (i + 1) * SUB, cols] = pieces[spots[j * 16 + i]].astype(F32)
-        out.append(pltpu.make_async_copy(weight.at[:, cols], made[4].at[:, cols], sems_out.at[4 + j]))
+        out.append(pltpu.make_async_copy(weight.at[:, cols], made[4].at[:, cols], sems.at[4 + j]))
         out[-1].start()
-        if j < 4:
-            into[j].wait()
-            out[j].start()
-    for j in range(tps * COLS // LANE, 4):
-        into[j].wait()
-        out[j].start()
     for copy in out:
         copy.wait()
 
@@ -584,7 +566,7 @@
     pair = [dma(2, n)] * 2
     relays = [dma(8, n)] * 2
     rowwise = [dma(2, 2, n)] * 2
-    keep = [vm(BF16, TOK, COLS)] * 4
+    in_vmem = pl.BlockSpec(memory_space=pltpu.VMEM)
     in_place = pl.BlockSpec(memory_space=pltpu.HBM)
     rest = FAR + tiles
     length = NEAR + rest
@@ -592,7 +574,6 @@
     scratch = [
         pltpu.SMEM(near_offsets.shape, jnp.int32), pltpu.SMEM(coupling.shape, jnp.int32),
         *(vm(BF16, *x.shape) for x in (queries, keys, values, out_weight, out_grad)), dma(7),
-        *keep, dma(5),
         vm(BF16, 2 * TOK, COLS), vm(BF16, 2 * TOK, COLS), vm(BF16, *pieces), vm(BF16, tps, TOK, COLS),
         vm(BF16, BLK, rest, COLS), vm(BF16, BLK, rest, COLS), vm(BF16, BLK * C1, tiles),
         vm(F32, BLK, length, COLS), vm(BF16, BLK, length, COLS), vm(BF16, TOK, COLS), vm(BF16, TOK, COLS), vm(F32, TOK, COLS),
@@ -607,18 +588,21 @@
     weight_grad = jax.ShapeDtypeStruct(out_weight.shape, F32)
     results = pl.pallas_call(
         functools.partial(kernel, n, tps, group),
-        out_shape=(*shapes, jax.ShapeDtypeStruct(pieces, BF16)),
+        out_shape=(*(pltpu.VMEM(x.shape, BF16) for x in shapes), pltpu.VMEM(pieces, BF16)),
         in_specs=[in_place] * 7,
-        out_specs=[in_place] * 5,
+        out_specs=[in_vmem] * 5,
         scratch_shapes=scratch,
         compiler_params=pltpu.CompilerParams(collective_id=0, has_side_effects=True, vmem_limit_bytes=VMEM),
-    )(near_offsets, coupling, queries, keys, values, out_weight, out_grad)
+    )(*(
+        pltpu.with_memory_space_constraint(x, pltpu.HBM)
+        for x in (near_offsets, coupling, queries, keys, values, out_weight, out_grad)
+    ))
     return pl.pallas_call(
         functools.partial(hand_over, n, tps),
         out_shape=(*shapes, weight_grad),
-        in_specs=[in_place] * 5,
+        in_specs=[in_vmem] * 5,
         out_specs=[in_place] * 5,
-        scratch_shapes=[*keep, vm(BF16, *pieces), vm(F32, *out_weight.shape), dma(5), dma(4 + tps * COLS // LANE)],
+        scratch_shapes=[vm(F32, *out_weight.shape), dma(4 + tps * COLS // LANE)],
         compiler_params=pltpu.CompilerParams(vmem_limit_bytes=VMEM),
     )(*results)
 

time: 71.9 us -> 64.4 us (0.90)
  the two profiles are of different devices: /device:TPU:6 before, /device:TPU:8 now
where the time goes in v3:
time: 64.4 us; the launch traced here: 64.2 us
  Pallas kernels  63.6 us (99%)
    pallas_call x1, Pallas kernels, shards(): pl.pallas_call(functools.partial(kernel, n, tps, group), out_shape=(*(plt...  62.4 us

profile of v3, /device:TPU:8, one launch (start us, length us, event | category | flops | bytes accessed | tf_op | source)
XLA Modules:
  0.0 64.2 jit_solution(1869879023463410737)
XLA Ops:
  0.6 62.4 %shard_map.110 = (bf16[256,256]{1,0:T(8,128)(2,1)S(1)}, bf16[256,256]{1,0:T(8,128)(2,1)S(1)}, bf16[256,256]{1,0:T(8,128)(2,1)S(1)}, bf16[256,256]{1,0:T(8,128)(2,1)S(1)}, bf16[128,16,128]{2,1,0:T(8,128)(2,1)S(1)}) custom-call(s32[4,3]{1,0:T(4,128)} %off_in.1, s32[4,16]{1,0:T(4,128)} %cpl_in.1, bf16[256,256]{1,0:T(8,128)(2,1)} %q_in.1, ...), custom_call_target="tpu_custom_call" | custom-call | tf_op jit(solution)/shard_map/pallas_call | solution.py:589
  63.0 1.2 %shard_map.111 = (bf16[256,256]{1,0:T(8,128)(2,1)}, bf16[256,256]{1,0:T(8,128)(2,1)}, bf16[256,256]{1,0:T(8,128)(2,1)}, bf16[256,256]{1,0:T(8,128)(2,1)}, f32[256,1024]{1,0:T(8,128)}) custom-call(bf16[256,256]{1,0:T(8,128)(2,1)S(1)} %get-tuple-element.10.refs_0_, bf16[256,256]{1,0:T(8,128)(2,1)S(1)} %get-tuple-element.11.refs_1_, ...), custom_call_target="tpu_custom_call" | custom-call | tf_op jit(solution)/shard_map/pallas_call | solution.py:600

commit v4 on v3

--- a/solution.py
+++ b/solution.py
@@ -22,10 +22,12 @@
 NEAR = 5 * NB
 FAR = C1 * BLK
 VMEM = 48 * 1024 * 1024
+SENDS, RECVS = 28, 36
 
 
 def each(low, high, body):
-    lax.fori_loop(low, high, lambda k, c: (body(low + high - 1 - k), c)[1], 0)
+    for k in range(high - 1, low - 1, -1):
+        body(k)
 
 
 def dot_nn(a, b):
@@ -57,11 +59,10 @@
         self.cross = self.y * (1 - self.xh) + self.z * self.xh
 
     def by(self, slot):
-        odd = lax.rem(slot, 2)
-        return odd * lax.div(slot + 1, 2) + (1 - odd) * (self.n - lax.div(slot, 2))
+        return (slot + 1) // 2 if slot % 2 else self.n - slot // 2
 
     def back(self, slot):
-        return slot + 2 * lax.rem(slot, 2) - 1 - lax.div(slot, self.n - 1)
+        return slot if slot == self.n - 1 else slot + 1 if slot % 2 else slot - 1
 
     def slot(self, ahead):
         n = self.n
@@ -110,61 +111,92 @@
     )
 
 
+class Log:
+    def __init__(self, w, sends, recvs):
+        self.w, self.sends, self.recvs = w, sends, recvs
+        self.flights, self.sent, self.received = [], 0, 0
+
+    def send(self):
+        self.sent += 1
+        return self.sends.at[self.sent - 1]
+
+    def recv(self):
+        self.received += 1
+        return self.recvs.at[self.received - 1]
+
+    def wait(self, size, send, recv):
+        return remote(size, size, send, recv, self.w.at(self.w.z, self.w.y, 1 - self.w.xh))
+
+
 class Flight:
-    def __init__(self, log, move, *args):
-        self.move, self.args = move, args
-        log.append(self)
+    def __init__(self, log, move, size, recv=None):
+        self.log, self.move, self.size = log, move, size
+        self.send, self.recv = log.send(), log.recv() if recv is None else recv
+        log.flights.append(self)
 
     def begin(self):
-        self.move(*self.args, lambda copy: copy.start())
+        self.move(lambda src, dst, device: remote(src, dst, self.send, self.recv, device).start())
 
     def land(self):
-        self.move(*self.args, lambda copy: copy.wait_recv())
+        self.log.wait(self.size, self.send, self.recv).wait_recv()
 
     def end(self):
-        self.move(*self.args, lambda copy: copy.wait_send())
-
-
-def spread(w, buf, send, recv, other, low, high, act):
-    own = buf.at[w.xh * w.n * w.n]
-
-    def one(i):
-        into = buf.at[w.xh * w.n * w.n + w.back(i)]
-        xh = 1 - w.xh if other else w.xh
-        act(remote(own, into, send.at[other, i], recv.at[other, w.back(i)], w.along_mine(i, xh)))
-
-    if low == 0:
-        if other:
-            act(remote(own, own, send.at[1, 0], recv.at[1, 0], w.at(w.z, w.y, 1 - w.xh)))
-        low = 1
-    each(low, high, one)
-
-
-def relay(w, buf, send, recv, batch, other, low, high, act):
-    n = w.n
-    base = (1 - w.xh if other else w.xh) * n * n
-
-    def one(i):
-        j = w.back(i)
-        mine = buf.at[pl.ds(base + low, high - low)]
-        into = buf.at[pl.ds(base + j * n + low, high - low)]
-        device = (w.along_mine if other else w.along_cross)(i, w.xh)
-        act(remote(mine, into, send.at[batch, i], recv.at[batch, j], device))
-
-    each(1, n, one)
+        self.log.wait(self.size, self.send, self.recv).wait_send()
+
+
+class Spread:
+    def __init__(self, log, w, buf, other, steps):
+        self.log, self.w, self.buf, self.other = log, w, buf, other
+        self.send = log.send()
+        self.recvs = {step: log.recv() for step in steps}
+        log.flights.append(self)
+
+    def count(self, low, high):
+        return high - max(low, 1) + (1 if self.other and low == 0 else 0)
+
+    def begin(self):
+        w = self.w
+        own = self.buf.at[w.xh * w.n * w.n]
+        xh = 1 - w.xh if self.other else w.xh
+        for i in range(w.n - 1, -1 if self.other else 0, -1):
+            j = w.back(i) if i else 0
+            recv = next(sem for (low, high), sem in self.recvs.items() if low <= j < high)
+            into = self.buf.at[w.xh * w.n * w.n + j]
+            device = w.along_mine(i, xh) if i else w.at(w.z, w.y, xh)
+            remote(own, into, self.send, recv, device).start()
+
+    def land(self, low, high):
+        size = self.buf.at[pl.ds(0, self.count(low, high))]
+        self.log.wait(size, self.send, self.recvs[low, high]).wait_recv()
+
+    def end(self):
+        size = self.buf.at[pl.ds(0, self.count(0, self.w.n))]
+        self.log.wait(size, self.send, next(iter(self.recvs.values()))).wait_send()
 
 
 class Gather:
-    def __init__(self, log, w, buf, s_1, r_1, s_2, r_2):
+    def __init__(self, log, w, buf):
         n = w.n
+        self.w, self.buf = w, buf
         cuts = [c for c in (1, 3, 5, 8) if c < n] + [n]
         same = list(zip([0] + cuts[:-1], cuts))
         cross = [(0, cuts[1])] + same[2:]
-        self.out = [Flight(log, spread, w, buf, s_1, r_1, 1, 0, n), Flight(log, spread, w, buf, s_1, r_1, 0, 0, n)]
-        steps = [(0, *part) for part in same] + [(1, *part) for part in cross]
-        steps.sort(key=lambda step: (step[1] + 2 * step[0], step[0]))
-        self.arrive = [Flight([], spread, w, buf, s_1, r_1, *step) for step in steps]
-        self.onward = [Flight(log, relay, w, buf, s_2, r_2, i, *step) for i, step in enumerate(steps)]
+        self.out = [Spread(log, w, buf, 0, same[1:]), Spread(log, w, buf, 1, cross)]
+        self.steps = [(0, *part) for part in same] + [(1, *part) for part in cross]
+        self.steps.sort(key=lambda step: (step[1] + 2 * step[0], step[0]))
+        self.onward = [self.relay(log, *step) for step in self.steps]
+
+    def relay(self, log, other, low, high):
+        w, n, buf = self.w, self.w.n, self.buf
+        base = (1 - w.xh if other else w.xh) * n * n
+        mine = buf.at[pl.ds(base + low, high - low)]
+
+        def move(copy):
+            for i in range(n - 1, 0, -1):
+                into = buf.at[pl.ds(base + w.back(i) * n + low, high - low)]
+                copy(mine, into, (w.along_mine if other else w.along_cross)(i, w.xh))
+
+        return Flight(log, move, buf.at[pl.ds(0, (n - 1) * (high - low))])
 
     def begin(self):
         self.out[1].begin()
@@ -172,8 +204,8 @@
         self.onward[0].begin()
 
     def forward(self):
-        for arrived, onward in zip(self.arrive[1:], self.onward[1:]):
-            arrived.land()
+        for (other, low, high), onward in zip(self.steps[1:], self.onward[1:]):
+            self.out[other].land(low, high)
             onward.begin()
 
     def land(self):
@@ -181,37 +213,38 @@
             onward.land()
 
 
-def to_rows(w, part, got, send, recv, batch, low, high, act):
-    n = w.n
-
-    def one(i):
-        for h, device in ((0, w.along_y(i)), (1, w.along_z(i))):
-            mine = part.at[pl.ds(h * n * n + i * n + low, high - low)]
-            act(remote(mine, got.at[h, i, pl.ds(low, high - low)], send.at[batch, h, i], recv.at[batch, h, i], device))
-
-    each(1, n, one)
-
-
-def to_owners(w, rows, got, send, recv, low, high, act):
-    def same(i):
-        act(remote(rows.at[w.xh, i], got.at[0, i], send.at[0, i], recv.at[0, i], w.along_mine(i, w.xh)))
-
-    def other(i):
-        act(remote(rows.at[1 - w.xh, i], got.at[1, i], send.at[1, i], recv.at[1, i], w.along_cross(i, 1 - w.xh)))
-
-    each(max(low, 1), high, same)
-    if low == 0:
-        act(remote(rows.at[1 - w.xh, 0], got.at[1, 0], send.at[1, 0], recv.at[1, 0], w.at(w.z, w.y, 1 - w.xh)))
-    each(max(low, 1), high, other)
-
-
 class Scatter:
-    def __init__(self, log, w, part, got_1, rows, got_2, s_1, r_1, s_2, r_2, cut):
+    def __init__(self, log, w, part, got_1, rows, got_2, cut):
         n = w.n
         self.w, self.part, self.got_1, self.rows, self.got_2 = w, part, got_1, rows, got_2
         self.cols = [(cut, n), (0, cut)] if cut else [(0, n)]
-        self.first = [Flight(log, to_rows, w, part, got_1, s_1, r_1, i, *c) for i, c in enumerate(self.cols)]
-        self.second = [Flight(log, to_owners, w, rows, got_2, s_2, r_2, *c) for c in self.cols]
+        self.first = [self.to_rows(log, *c) for c in self.cols]
+        self.second = [self.to_owners(log, *c) for c in self.cols]
+
+    def to_rows(self, log, low, high):
+        w, n = self.w, self.w.n
+
+        def move(copy):
+            for i in range(n - 1, 0, -1):
+                for h, device in ((0, w.along_y(i)), (1, w.along_z(i))):
+                    mine = self.part.at[pl.ds(h * n * n + i * n + low, high - low)]
+                    copy(mine, self.got_1.at[h, i, pl.ds(low, high - low)], device)
+
+        return Flight(log, move, self.part.at[pl.ds(0, 2 * (n - 1) * (high - low))])
+
+    def to_owners(self, log, low, high):
+        w = self.w
+
+        def move(copy):
+            for i in range(high - 1, max(low, 1) - 1, -1):
+                copy(self.rows.at[1 - w.xh, i], self.got_2.at[1, i], w.along_cross(i, 1 - w.xh))
+            if low == 0:
+                copy(self.rows.at[1 - w.xh, 0], self.got_2.at[1, 0], w.at(w.z, w.y, 1 - w.xh))
+            for i in range(high - 1, max(low, 1) - 1, -1):
+                copy(self.rows.at[w.xh, i], self.got_2.at[0, i], w.along_mine(i, w.xh))
+
+        count = 2 * (high - max(low, 1)) + (1 if low == 0 else 0)
+        return Flight(log, move, self.part.at[pl.ds(0, count)])
 
     def begin(self):
         for first in self.first:
@@ -247,15 +280,31 @@
     kpad, vpad, fine, ogs, kft, vft, hot, probs, halves, att, gatt, mine_out,
     msend, mgot, gkpad, gvpad, hsend, hgot, dlist, dtop,
     wpart, wgot1, wrows, wgot2, wfull, fpart, fgot1, frows, fgot2,
-    s_h, r_h, s_o, r_o, s_m, r_m, s_b, r_b,
-    s_g1, r_g1, s_g2, r_g2, s_w1, r_w1, s_w2, r_w2, s_w3, r_w3, s_w4, r_w4, s_f1, r_f1, s_f2, r_f2,
+    sends, recvs,
 ):
     w = Place(n, tps)
     tiles = w.seqs
     groups = tiles // group
     nblk = tiles * BLK
     half = TOK // 2
-    flights = []
+    log = Log(w, sends, recvs)
+
+    barrier = pltpu.get_barrier_semaphore()
+
+    def greet(device):
+        pl.semaphore_signal(barrier, inc=1, device_id=device, device_id_type=MESH)
+
+    def greet_square(i):
+        greet(w.along_y(i))
+        greet(w.along_z(i))
+        greet(w.along_mine(i, 1 - w.xh))
+        greet(w.along_cross(i, 1 - w.xh))
+
+    each(1, n, greet_square)
+    greet(w.at(w.z, w.y, 1 - w.xh))
+    greet(w.step(1))
+    greet(w.step(-1))
+    each(1, tps, lambda k: greet(w.tp_at(k)[1]))
 
     brought = [
         pltpu.make_async_copy(src, dst, s_in.at[i])
@@ -265,23 +314,6 @@
     ]
     for copy in brought:
         copy.start()
-
-    barrier = pltpu.get_barrier_semaphore()
-
-    def greet(device):
-        pl.semaphore_signal(barrier, inc=1, device_id=device, device_id_type=MESH)
-
-    def greet_square(i):
-        greet(w.along_y(i))
-        greet(w.along_z(i))
-        greet(w.along_mine(i, 1 - w.xh))
-        greet(w.along_cross(i, 1 - w.xh))
-
-    each(1, n, greet_square)
-    greet(w.at(w.z, w.y, 1 - w.xh))
-    greet(w.step(1))
-    greet(w.step(-1))
-    each(1, tps, lambda k: greet(w.tp_at(k)[1]))
 
     for copy in brought[:2]:
         copy.wait()
@@ -294,20 +326,18 @@
     fine[w.xh * n * n] = (piece * 0.125).astype(BF16)
     pl.semaphore_wait(barrier, 4 * (n - 1) + 3 + tps - 1)
 
-    def move_halo(act):
-        for i, (src, pad) in enumerate(((k_ref, kpad), (v_ref, vpad))):
-            act(remote(src.at[pl.ds(half, half)], pad.at[pl.ds(0, half)], s_h.at[i], r_h.at[i], w.step(1)))
-            act(remote(src.at[pl.ds(0, half)], pad.at[pl.ds(half + TOK, half)], s_h.at[2 + i], r_h.at[2 + i], w.step(-1)))
-
-    def move_columns(act):
-        def one(k):
-            act(remote(og_ref, ogs.at[w.tp], s_o.at[k], r_o.at[k], w.tp_at(k)[1]))
-
-        each(1, tps, one)
-
-    summaries = Gather(flights, w, fine, s_g1, r_g1, s_g2, r_g2)
-    halo = Flight(flights, move_halo)
-    columns = Flight(flights, move_columns)
+    def move_halo(copy):
+        for src, pad in ((k_ref, kpad), (v_ref, vpad)):
+            copy(src.at[pl.ds(half, half)], pad.at[pl.ds(0, half)], w.step(1))
+            copy(src.at[pl.ds(0, half)], pad.at[pl.ds(half + TOK, half)], w.step(-1))
+
+    def move_columns(copy):
+        for k in range(1, tps):
+            copy(og_ref, ogs.at[w.tp], w.tp_at(k)[1])
+
+    summaries = Gather(log, w, fine)
+    halo = Flight(log, move_halo, kpad)
+    columns = Flight(log, move_columns, ogs.at[pl.ds(0, tps - 1)])
     summaries.begin()
     halo.begin()
     brought[2].wait()
@@ -370,6 +400,13 @@
 
     spots = w.spots()
     halo.land()
+    for b in range(BLK):
+        scores = dot_nt(kpad[b * NB : b * NB + NEAR], diagonal(q_ref[b * NB : (b + 1) * NB])) * 0.125
+        for d in range(5):
+            target = w.seq * BLK + b + d - 2
+            chosen = (off_ref[b, 0] == d - 2) | (off_ref[b, 1] == d - 2) | (off_ref[b, 2] == d - 2)
+            usable = chosen & (target >= 0) & (target < nblk)
+            probs[b, d * NB : (d + 1) * NB] = scores[d * NB : (d + 1) * NB] + jnp.where(usable, 0.0, -1e30)
     summaries.land()
 
     packed = jnp.concatenate([fine[g * group : (g + 1) * group].reshape(size, LANE) for g in range(groups)], 1)
@@ -403,16 +440,9 @@
         return jnp.concatenate([pad[b * NB : b * NB + NEAR], rest[b]], 0)
 
     for b in range(BLK):
-        keys = listed_rows(kpad, kft, b)
         vals = listed_rows(vpad, vft, b)
-        scores = dot_nt(keys, diagonal(q_ref[b * NB : (b + 1) * NB])) * 0.125
-        parts = []
-        for d in range(5):
-            target = w.seq * BLK + b + d - 2
-            chosen = (off_ref[b, 0] == d - 2) | (off_ref[b, 1] == d - 2) | (off_ref[b, 2] == d - 2)
-            usable = chosen & (target >= 0) & (target < nblk)
-            parts.append(scores[d * NB : (d + 1) * NB] + jnp.where(usable, 0.0, -1e30))
-        scores = jnp.concatenate(parts + [scores[NEAR:]], 0)
+        rest = dot_nt(kft[b], diagonal(q_ref[b * NB : (b + 1) * NB])) * 0.125
+        scores = jnp.concatenate([probs[b, :NEAR], rest], 0)
         peak = jnp.max(scores, 0, keepdims=True)
         exps = jnp.exp(scores - peak)
         prob = exps * (1.0 / jnp.sum(exps, 0, keepdims=True))
@@ -427,21 +457,19 @@
         for j in range(COLS // LANE):
             for i in range(TOK // SUB):
                 wpart[spots[(t * 2 + j) * 16 + i]] = part[i * SUB : (i + 1) * SUB, j * LANE : (j + 1) * LANE]
-    weight = Scatter(flights, w, wpart, wgot1, wrows, wgot2, s_w1, r_w1, s_w2, r_w2, 5 if n == 8 else n - 1)
-    whole = Gather(flights, w, wfull, s_w3, r_w3, s_w4, r_w4)
+    weight = Scatter(log, w, wpart, wgot1, wrows, wgot2, 5 if n == 8 else n - 1)
+    whole = Gather(log, w, wfull)
     weight.begin()
 
     for t in range(tps):
         msend[t] = dot_nn(att[...], w_ref[:, t * COLS : (t + 1) * COLS]).astype(BF16)
 
-    def move_mix(act):
-        def one(k):
+    def move_mix(copy):
+        for k in range(1, tps):
             c, device = w.tp_at(k)
-            act(remote(msend.at[c], mgot.at[k], s_m.at[k], r_m.at[k], device))
-
-        each(1, tps, one)
-
-    mix = Flight(flights, move_mix)
+            copy(msend.at[c], mgot.at[k], device)
+
+    mix = Flight(log, move_mix, mgot.at[pl.ds(0, tps - 1)])
     mix.begin()
     mine_out[...] = dot_nn(att[...], w_ref[:, pl.ds(pl.multiple_of(w.tp * COLS, COLS), COLS)])
 
@@ -478,10 +506,10 @@
         hsend[i] = pad[half + TOK :].astype(BF16)
         hsend[2 + i] = pad[:half].astype(BF16)
 
-    def move_back(act):
+    def move_back(copy):
         for i in range(2):
-            act(remote(hsend.at[i], hgot.at[i], s_b.at[i], r_b.at[i], w.step(1)))
-            act(remote(hsend.at[2 + i], hgot.at[2 + i], s_b.at[2 + i], r_b.at[2 + i], w.step(-1)))
+            copy(hsend.at[i], hgot.at[i], w.step(1))
+            copy(hsend.at[2 + i], hgot.at[2 + i], w.step(-1))
 
     tile_grad = dot_tn(hot[...], dlist[...])
     cols = []
@@ -499,9 +527,9 @@
     packed = dot_nn(swap_back, by_row).astype(BF16)
     for g in range(groups):
         fpart[g * group : (g + 1) * group] = packed[:, g * LANE : (g + 1) * LANE].reshape(group, SUB, LANE)
-    halo_back = Flight(flights, move_back)
+    halo_back = Flight(log, move_back, hgot)
     halo_back.begin()
-    coupled = Scatter(flights, w, fpart, fgot1, frows, fgot2, s_f1, r_f1, s_f2, r_f2, 0)
+    coupled = Scatter(log, w, fpart, fgot1, frows, fgot2, 0)
 
     weight.forward()
     coupled.begin()
@@ -532,7 +560,7 @@
                     rows[:, c * LANE : (c + 1) * LANE] + fine_grad[s : s + 1]
                 ).astype(BF16)
 
-    for flight in flights:
+    for flight in log.flights:
         if flight not in whole.onward:
             flight.end()
     whole.land()
@@ -563,9 +591,6 @@
     pieces = (tiles, SUB, LANE)
     dma = lambda *shape: pltpu.SemaphoreType.DMA(shape)
     vm = lambda dtype, *shape: pltpu.VMEM(shape, dtype)
-    pair = [dma(2, n)] * 2
-    relays = [dma(8, n)] * 2
-    rowwise = [dma(2, 2, n)] * 2
     in_vmem = pl.BlockSpec(memory_space=pltpu.VMEM)
     in_place = pl.BlockSpec(memory_space=pltpu.HBM)
     rest = FAR + tiles
@@ -580,8 +605,7 @@
         vm(BF16, tps, TOK, COLS), vm(BF16, tps, TOK, COLS), vm(F32, 2 * TOK, COLS), vm(F32, 2 * TOK, COLS),
         vm(BF16, 4, TOK // 2, COLS), vm(BF16, 4, TOK // 2, COLS), vm(BF16, BLK * C1, SUB * LANE), vm(F32, tiles, 2 * COLS),
         *sums, vm(BF16, *pieces), *sums,
-        dma(4), dma(4), dma(tps), dma(tps), dma(tps), dma(tps), dma(4), dma(4),
-        *pair, *relays, *rowwise, *pair, *pair, *relays, *rowwise, *pair,
+        dma(SENDS), dma(RECVS),
     ]
     like = lambda x: jax.ShapeDtypeStruct(x.shape, BF16)
     shapes = (like(out_grad), like(queries), like(keys), like(values))

time: 64.4 us -> 59.4 us (0.922)
  the two profiles are of different devices: /device:TPU:8 before, /device:TPU:6 now
where the time goes in v4:
time: 59.4 us; the launch traced here: 59.2 us
  Pallas kernels  58.6 us (99%)
  between operations  0.64 us (1%)
    pallas_call x1, Pallas kernels, shards(): pl.pallas_call(functools.partial(kernel, n, tps, group), out_shape=(*(plt...  57.3 us
    pallas_call x1, Pallas kernels, shards(): pl.pallas_call(functools.partial(hand_over, n, tps), out_shape=(*shapes,...  1.24 us

profile of v4, /device:TPU:6, one launch (start us, length us, event | category | flops | bytes accessed | tf_op | source)
XLA Modules:
  0.0 59.2 jit_solution(11296669128733627009)
XLA Ops:
  0.6 57.3 %shard_map.110 = (bf16[256,256]{1,0:T(8,128)(2,1)S(1)}, bf16[256,256]{1,0:T(8,128)(2,1)S(1)}, bf16[256,256]{1,0:T(8,128)(2,1)S(1)}, bf16[256,256]{1,0:T(8,128)(2,1)S(1)}, bf16[128,16,128]{2,1,0:T(8,128)(2,1)S(1)}) custom-call(s32[4,3]{1,0:T(4,128)} %off_in.1, s32[4,16]{1,0:T(4,128)} %cpl_in.1, bf16[256,256]{1,0:T(8,128)(2,1)} %q_in.1, ...), custom_call_target="tpu_custom_call" | custom-call | tf_op jit(solution)/shard_map/pallas_call | solution.py:613
  58.0 1.2 %shard_map.111 = (bf16[256,256]{1,0:T(8,128)(2,1)}, bf16[256,256]{1,0:T(8,128)(2,1)}, bf16[256,256]{1,0:T(8,128)(2,1)}, bf16[256,256]{1,0:T(8,128)(2,1)}, f32[256,1024]{1,0:T(8,128)}) custom-call(bf16[256,256]{1,0:T(8,128)(2,1)S(1)} %get-tuple-element.10.refs_0_, bf16[256,256]{1,0:T(8,128)(2,1)S(1)} %get-tuple-element.11.refs_1_, ...), custom_call_target="tpu_custom_call" | custom-call | tf_op jit(solution)/shard_map/pallas_call | solution.py:624

commit v5 on v4

--- a/solution.py
+++ b/solution.py
@@ -22,7 +22,7 @@
 NEAR = 5 * NB
 FAR = C1 * BLK
 VMEM = 48 * 1024 * 1024
-SENDS, RECVS = 28, 36
+SENDS, RECVS = 22, 26
 
 
 def each(low, high, body):
@@ -178,7 +178,7 @@
     def __init__(self, log, w, buf):
         n = w.n
         self.w, self.buf = w, buf
-        cuts = [c for c in (1, 3, 5, 8) if c < n] + [n]
+        cuts = [c for c in (1, 5, 8) if c < n] + [n]
         same = list(zip([0] + cuts[:-1], cuts))
         cross = [(0, cuts[1])] + same[2:]
         self.out = [Spread(log, w, buf, 0, same[1:]), Spread(log, w, buf, 1, cross)]
@@ -457,7 +457,7 @@
         for j in range(COLS // LANE):
             for i in range(TOK // SUB):
                 wpart[spots[(t * 2 + j) * 16 + i]] = part[i * SUB : (i + 1) * SUB, j * LANE : (j + 1) * LANE]
-    weight = Scatter(log, w, wpart, wgot1, wrows, wgot2, 5 if n == 8 else n - 1)
+    weight = Scatter(log, w, wpart, wgot1, wrows, wgot2, 0)
     whole = Gather(log, w, wfull)
     weight.begin()
 
@@ -534,17 +534,17 @@
     weight.forward()
     coupled.begin()
 
+    wfull[w.xh * n * n] = weight.land().astype(BF16)
+    whole.begin()
+    coupled.forward()
+    whole.forward()
+
     mix.land()
     total = mine_out[...]
     for k in range(1, tps):
         total += mgot[k].astype(F32)
     mixed_ref[...] = total.astype(BF16)
     halo_back.land()
-
-    wfull[w.xh * n * n] = weight.land().astype(BF16)
-    whole.begin()
-    coupled.forward()
-    whole.forward()
 
     fine_grad = coupled.land() * 0.125
     for i, (pad, out) in enumerate(((gkpad, gk_ref), (gvpad, gv_ref))):

time: 59.4 us -> 59.3 us (level)
  the two profiles are of different devices: /device:TPU:6 before, /device:TPU:8 now
where the time goes in v5:
time: 59.3 us; the launch traced here: 59.1 us
  Pallas kernels  58.5 us (99%)
  between operations  0.64 us (1%)
    pallas_call x1, Pallas kernels, shards(): pl.pallas_call(functools.partial(kernel, n, tps, group), out_shape=(*(plt...  57.3 us
    pallas_call x1, Pallas kernels, shards(): pl.pallas_call(functools.partial(hand_over, n, tps), out_shape=(*shapes,...  1.24 us

profile of v5, /device:TPU:8, one launch (start us, length us, event | category | flops | bytes accessed | tf_op | source)
XLA Modules:
  0.0 59.1 jit_solution(11837763981034387876)
XLA Ops:
  0.6 57.3 %shard_map.110 = (bf16[256,256]{1,0:T(8,128)(2,1)S(1)}, bf16[256,256]{1,0:T(8,128)(2,1)S(1)}, bf16[256,256]{1,0:T(8,128)(2,1)S(1)}, bf16[256,256]{1,0:T(8,128)(2,1)S(1)}, bf16[128,16,128]{2,1,0:T(8,128)(2,1)S(1)}) custom-call(s32[4,3]{1,0:T(4,128)} %off_in.1, s32[4,16]{1,0:T(4,128)} %cpl_in.1, bf16[256,256]{1,0:T(8,128)(2,1)} %q_in.1, ...), custom_call_target="tpu_custom_call" | custom-call | tf_op jit(solution)/shard_map/pallas_call | solution.py:613
  57.9 1.2 %shard_map.111 = (bf16[256,256]{1,0:T(8,128)(2,1)}, bf16[256,256]{1,0:T(8,128)(2,1)}, bf16[256,256]{1,0:T(8,128)(2,1)}, bf16[256,256]{1,0:T(8,128)(2,1)}, f32[256,1024]{1,0:T(8,128)}) custom-call(bf16[256,256]{1,0:T(8,128)(2,1)S(1)} %get-tuple-element.10.refs_0_, bf16[256,256]{1,0:T(8,128)(2,1)S(1)} %get-tuple-element.11.refs_1_, ...), custom_call_target="tpu_custom_call" | custom-call | tf_op jit(solution)/shard_map/pallas_call | solution.py:624
